TPU v7x, 512 devices: a whole 4x8x8 slice. The times are simulated.
512 devices in a mesh: dp: 8 (over y_hi, core), domain: 64 (over y_lo, x, z).
Axes of the slice: x: 4, y: 8 (y_hi: 4, y_lo: 2; y = y_hi * 2 + y_lo), z: 8, core: 2. Of those that a mesh axis runs over, the one named last changes fastest.
Arguments:
- inputs: bfloat16 [8, 192, 64, 2304], P('dp', 'domain'), may hold values from -6 to 6
- preact: bfloat16 [8, 192, 64, 2304], P('dp', 'domain'), may hold values from -4 to 4
- spectral_weight: bfloat16 [128, 256, 64, 128], P('dp', 'domain'), may hold values from -6 to 6
- point_weight: bfloat16 [64, 64], replicated, may hold values from -0.75 to 0.75
- readout: float32 [48, 2, 64], replicated, may hold values from -0.75 to 0.75
- observed: float32 [8, 2, 32768], P('dp', None, 'domain'), may hold values from -4 to 4
- cell_index: int32 [8, 32768], P('dp', 'domain'), may hold values from 0 to 6911
- drift_steps: int32 [8, 32768], P('dp', 'domain'), may hold values from 0 to 47
- counts: int32 [8, 64], P('dp', 'domain'), may hold values from 1 to 512, as said below
Outputs:
- input_grad: bfloat16 [8, 192, 64, 2304], P('dp', 'domain')
- weight_grad: bfloat16 [128, 256, 64, 128], P('dp', 'domain')
Inputs may be any that keep to these rules, and one draw needn't show every extreme that they name: `counts`: for every case some slab has exactly 512 live slots; slots at or beyond a slab's count carry no loss. `cell_index`: cell within the slab: row within the slab times 2304 plus longitude.
All inputs are finite; a program needn't handle non-finite values.
Results may differ from a plain program's by a relative error of at most 0.025.
Values may be sent and summed in bfloat16 or wider, within the bound.
No kernel may reach another device: no remote copies, remote signals or barrier semaphores. Data moves between devices by JAX's collectives and lax.ppermute only.
A program may use at most 64 MiB of HBM per device.

v0:
```python
import jax
import jax.numpy as jnp
from jax import lax
from jax.sharding import PartitionSpec as P

NX = 2304
NY = 2160
KX = 256
KY = 128
STEPS = 48
SLOTS = 512


two_pi = 6.283185307179586
loss_scale = 8.0


def gelu_fn(value):
    return jax.nn.gelu(value, approximate=True)


def lon_table(kx_local):
    column = jnp.arange(2 * KX, dtype=jnp.int32)
    block = column // (2 * kx_local)
    which = column // kx_local % 2
    wavenum = block * kx_local + column % kx_local
    points = jnp.arange(NX, dtype=jnp.int32)
    phase = (points[:, None] * wavenum[None, :] % NX).astype(jnp.float32) * (two_pi / NX)
    cosine = jnp.cos(phase).astype(jnp.bfloat16)
    minus_sine = (-jnp.sin(phase)).astype(jnp.bfloat16)
    return jnp.where(which[None, :] == 0, cosine, minus_sine)


def lat_table(window_rows):
    index_q = jnp.arange(KY, dtype=jnp.int32)
    wavenum = jnp.where(index_q < KY // 2, index_q, NY - KY + index_q)
    rows_y = jnp.arange(window_rows, dtype=jnp.int32) * (NY // window_rows)
    phase = (wavenum[:, None] * rows_y[None, :] % NY).astype(jnp.float32) * (two_pi / NY)
    return jnp.concatenate(
        [jnp.cos(phase).astype(jnp.bfloat16), jnp.sin(phase).astype(jnp.bfloat16)], axis=0
    )


def loss_field(preact, readout, observed, cell_index, drift_steps, counts):
    case_count = preact.shape[0]
    live = (jnp.arange(SLOTS, dtype=jnp.int32)[None, :] < counts).astype(jnp.float32)
    row_of = cell_index // NX
    col_of = cell_index % NX
    case_idx = jnp.broadcast_to(jnp.arange(case_count, dtype=jnp.int32)[:, None], cell_index.shape)
    zslot = preact[case_idx, row_of, :, col_of].astype(jnp.float32)
    onehot = (drift_steps[..., None] == jnp.arange(STEPS, dtype=jnp.int32)).astype(jnp.float32)
    chosen = jnp.einsum("nes,sjc->nejc", onehot, readout)
    activated, pullback = jax.vjp(gelu_fn, zslot)
    velocity = jnp.einsum("nejc,nec->nej", chosen, activated)
    misfit = loss_scale * live[..., None] * (velocity - jnp.transpose(observed, (0, 2, 1)))
    dslot = pullback(jnp.einsum("nejc,nej->nec", chosen, misfit))[0]
    dgrid = jnp.zeros(preact.shape, jnp.float32).at[case_idx, row_of, :, col_of].add(dslot)
    return dgrid.astype(jnp.bfloat16)


def lon_forward(field, table):
    case_count, lat_rows, channels, width = field.shape
    spectra = jnp.dot(field.reshape(-1, width), table, preferred_element_type=jnp.float32)
    return spectra.astype(jnp.bfloat16).reshape(case_count, lat_rows, channels, table.shape[1])


def lat_forward(spectra, stacked, factor):
    case_count, rows_y, channels, columns = spectra.shape
    kx_local = columns // 2
    flat = spectra.reshape(case_count, rows_y, channels * columns)
    both = jnp.einsum("qy,nym->nqm", stacked, flat, preferred_element_type=jnp.float32)
    both = both.reshape(case_count, 2, KY, channels, 2, kx_local)
    cos_part = both[:, 0]
    sin_part = both[:, 1]
    real_part = (cos_part[:, :, :, 0] + sin_part[:, :, :, 1]) * factor
    imag_part = (cos_part[:, :, :, 1] - sin_part[:, :, :, 0]) * factor
    modes = jnp.stack([real_part, imag_part], axis=3).astype(jnp.bfloat16)
    return modes.reshape(case_count, KY, channels * columns)


def local(
    inputs,
    preact,
    spectral_weight,
    point_weight,
    readout,
    observed,
    cell_index,
    drift_steps,
    counts,
):
    case_count, lat_rows, channels, width = inputs.shape
    parts = lax.axis_size("domain")
    window_rows = lat_rows * parts
    kx_local = KX // parts
    ky_local = spectral_weight.shape[0]
    table = lon_table(kx_local)
    stacked = lat_table(window_rows)
    ones = jnp.ones((kx_local,), jnp.float32)
    wavenum = lax.axis_index("domain") * kx_local + jnp.arange(kx_local, dtype=jnp.int32)
    mscale = jnp.where(wavenum == 0, 1.0, 2.0).astype(jnp.float32) / (NX * window_rows)
    dz = loss_field(preact, readout, observed, cell_index, drift_steps, counts)
    input_spec = lon_forward(inputs, table)
    loss_spec = lon_forward(dz, table)
    input_spec, loss_spec = (
        lax.all_to_all(input_spec, "domain", split_axis=3, concat_axis=1, tiled=True),
        lax.all_to_all(loss_spec, "domain", split_axis=3, concat_axis=1, tiled=True),
    )
    input_modes = lat_forward(input_spec, stacked, ones)
    loss_modes = lat_forward(loss_spec, stacked, mscale)
    input_modes, loss_modes = (
        lax.all_to_all(input_modes, "dp", split_axis=1, concat_axis=0, tiled=True),
        lax.all_to_all(loss_modes, "dp", split_axis=1, concat_axis=0, tiled=True),
    )
    all_cases = input_modes.shape[0]
    shape5 = (all_cases, ky_local, channels, 2, kx_local)
    xmodes = input_modes.reshape(shape5)
    ymodes = loss_modes.reshape(shape5)
    x_real, x_imag = (xmodes[:, :, :, 0], xmodes[:, :, :, 1])
    y_real, y_imag = (ymodes[:, :, :, 0], ymodes[:, :, :, 1])
    w_real = spectral_weight[..., :channels]
    w_imag = spectral_weight[..., channels:]
    f32 = jnp.float32
    grad_real = jnp.einsum("nqcj,nqoj->qjco", x_real, y_real, preferred_element_type=f32)
    grad_real = grad_real + jnp.einsum(
        "nqcj,nqoj->qjco", x_imag, y_imag, preferred_element_type=f32
    )
    grad_imag = jnp.einsum("nqcj,nqoj->qjco", x_real, y_imag, preferred_element_type=f32)
    grad_imag = grad_imag - jnp.einsum(
        "nqcj,nqoj->qjco", x_imag, y_real, preferred_element_type=f32
    )
    weight_grad = jnp.concatenate([grad_real, grad_imag], axis=-1).astype(jnp.bfloat16)
    back_real = jnp.einsum("qjco,nqoj->nqcj", w_real, y_real, preferred_element_type=f32)
    back_real = back_real + jnp.einsum(
        "qjco,nqoj->nqcj", w_imag, y_imag, preferred_element_type=f32
    )
    back_imag = jnp.einsum("qjco,nqoj->nqcj", w_real, y_imag, preferred_element_type=f32)
    back_imag = back_imag - jnp.einsum(
        "qjco,nqoj->nqcj", w_imag, y_real, preferred_element_type=f32
    )
    back_modes = jnp.stack([back_real, back_imag], axis=3).astype(jnp.bfloat16)
    back_modes = back_modes.reshape(all_cases, ky_local, channels * 2 * kx_local)
    back_modes = lax.all_to_all(back_modes, "dp", split_axis=0, concat_axis=1, tiled=True)
    cos_y = stacked[:KY]
    sin_y = stacked[KY:]
    with_cos = jnp.einsum("qy,nqm->nym", cos_y, back_modes, preferred_element_type=f32)
    with_sin = jnp.einsum("qy,nqm->nym", sin_y, back_modes, preferred_element_type=f32)
    with_cos = with_cos.reshape(case_count, window_rows, channels, 2, kx_local)
    with_sin = with_sin.reshape(case_count, window_rows, channels, 2, kx_local)
    lat_real = with_cos[:, :, :, 0] - with_sin[:, :, :, 1]
    lat_imag = with_cos[:, :, :, 1] + with_sin[:, :, :, 0]
    synth = jnp.stack([lat_real, lat_imag], axis=3).astype(jnp.bfloat16)
    synth = synth.reshape(case_count, window_rows, channels, 2 * kx_local)
    synth = lax.all_to_all(synth, "domain", split_axis=1, concat_axis=3, tiled=True)
    spectral = jnp.dot(synth.reshape(-1, 2 * KX), table.T, preferred_element_type=f32)
    spectral = spectral.reshape(case_count, lat_rows, channels, width)
    pointwise = jnp.einsum("nlox,co->nlcx", dz, point_weight, preferred_element_type=f32)
    input_grad = (spectral + pointwise).astype(jnp.bfloat16)
    return (input_grad, weight_grad)


def solution(mesh):
    placed = (
        P("dp", "domain", None, None),
        P("dp", "domain", None, None),
        P("dp", "domain", None, None),
        P(),
        P(),
        P("dp", None, "domain"),
        P("dp", "domain"),
        P("dp", "domain"),
        P("dp", "domain"),
    )
    return jax.shard_map(
        local,
        mesh=mesh,
        in_specs=placed,
        out_specs=(P("dp", "domain", None, None), P("dp", "domain", None, None)),
        check_vma=False,
    )
```

profile of v0, /device:TPU:8, one launch (start us, length us, event | category | flops | bytes accessed | tf_op | source)
XLA Modules:
  0.0 265.5 jit_solution(15535520265123058970)
XLA Ops:
  1.6 1.9 copy.118
  3.5 3.1 %gather_fusion = bf16[512,64]{1,0:T(8,128)(2,1)S(1)} fusion(bf16[1,3,64,2304]{2,3,1,0:T(8,128)(2,1)S(1)} %copy.118, s32[512]{0:T(512)S(1)} %bitcast.171), kind=kCustom, calls=%fused_computation | custom fusion | bytes 137216 | tf_op jit(solution)/shard_map/gather | solution.py:50
  8.0 2.0 broadcast.280
  10.0 51.1 %scatter_fusion = f32[3,64,2304]{1,2,0:T(8,128)} fusion(f32[3,64,2304]{1,2,0:T(8,128)} %broadcast.280, s32[512]{0:T(512)S(1)} %bitcast.170, f32[512,64]{1,0:T(8,128)S(1)} %copy.120), kind=kCustom, calls=%fused_computation.1 | custom fusion | flops 32768 | bytes 397312 | tf_op jit(solution)/shard_map/scatter-add | solution.py:57
  61.2 2.4 copy.121
  63.5 19.9 %fusion.14 = bf16[192,512]{1,0:T(8,128)(2,1)S(1)} fusion(bf16[192,2304]{1,0:T(8,128)(2,1)S(1)} %bitcast.173, s32[512]{0:T(512)S(1)} %fusion.84, pred[512]{0:T(512)(128)(4,1)S(1)} %fusion.81), kind=kOutput, calls=%fused_computation.25 | convolution fusion | flops 468418560 | bytes 1083904 | tf_op jit(solution)/shard_map/dot_general | solution.py:63
  84.8 15.2 %all-to-all-start = ((bf16[64,2,768]{2,1,0:T(2,128)(2,1)}), bf16[64,2,768]{2,1,0:T(2,128)(2,1)S(1)}, u32[]{:S(2)}, u32[]{:S(2)}) async-start(bf16[64,2,768]{2,1,0:T(2,128)(2,1)} %reshape.359), calls=%async_computation | async-start | bytes 393216 | tf_op jit(solution)/shard_map/all_to_all | solution.py:107
  100.0 19.7 %fusion.17 = bf16[512,192]{0,1:T(8,128)(2,1)S(1)} fusion(bf16[192,2304]{1,0:T(8,128)(2,1)S(1)} %bitcast.169, s32[512]{0:T(512)S(1)} %fusion.84, pred[512]{0:T(512)(128)(4,1)S(1)} %fusion.81), kind=kOutput, calls=%fused_computation.26 | convolution fusion | flops 468418560 | bytes 1083904 | tf_op jit(solution)/shard_map/dot_general | solution.py:63
  121.8 11.3 %all-to-all-start.4 = ((bf16[64,2,768]{2,1,0:T(2,128)(2,1)}), bf16[64,2,768]{2,1,0:T(2,128)(2,1)S(1)}, u32[]{:S(2)}, u32[]{:S(2)}) async-start(bf16[64,2,768]{2,1,0:T(2,128)(2,1)} %reshape.365), calls=%async_computation.4 | async-start | bytes 393216 | tf_op jit(solution)/shard_map/all_to_all | solution.py:106
  133.5 2.8 %copy.124 = bf16[1,64,3,64,8]{4,3,2,1,0:T(8,128)(2,1)} copy(bf16[1,64,3,64,8]{3,4,1,2,0:T(8,128)(2,1)S(1)} %bitcast.180) | data formatting | bytes 393216 | tf_op jit(solution)/shard_map/all_to_all | solution.py:107
  136.2 5.6 %reshape.313 = bf16[192,512]{1,0:T(8,128)(2,1)S(1)} reshape(bf16[1,64,3,64,8]{4,3,2,1,0:T(8,128)(2,1)} %copy.124) | data formatting | bytes 393216 | tf_op jit(solution)/shard_map/reshape.14
  145.8 6.2 %all-to-all-start.1 = ((bf16[8,2,4096]{2,1,0:T(2,128)(2,1)}), bf16[8,2,4096]{2,1,0:T(2,128)(2,1)S(1)}, u32[]{:S(2)}, u32[]{:S(2)}) async-start(bf16[8,2,4096]{2,1,0:T(2,128)(2,1)} %reshape.361), calls=%async_computation.1 | async-start | bytes 262144 | tf_op jit(solution)/shard_map/all_to_all | solution.py:113
  152.4 2.8 %copy.141 = bf16[1,64,3,64,8]{4,3,2,1,0:T(8,128)(2,1)} copy(bf16[1,64,3,64,8]{3,4,1,2,0:T(8,128)(2,1)S(1)} %bitcast.181) | data formatting | bytes 393216 | tf_op jit(solution)/shard_map/all_to_all | solution.py:106
  155.2 5.6 %reshape.323 = bf16[192,512]{1,0:T(8,128)(2,1)S(1)} reshape(bf16[1,64,3,64,8]{4,3,2,1,0:T(8,128)(2,1)} %copy.141) | data formatting | bytes 393216 | tf_op jit(solution)/shard_map/reshape.53
  164.2 7.4 %all-to-all-start.5 = ((bf16[8,2,4096]{2,1,0:T(2,128)(2,1)}), bf16[8,2,4096]{2,1,0:T(2,128)(2,1)S(1)}, u32[]{:S(2)}, u32[]{:S(2)}) async-start(bf16[8,2,4096]{2,1,0:T(2,128)(2,1)} %reshape.367), calls=%async_computation.5 | async-start | bytes 262144 | tf_op jit(solution)/shard_map/all_to_all | solution.py:112
  174.1 6.7 %all-to-all-done.5 = bf16[8,2,4096]{2,1,0:T(2,128)(2,1)S(1)} async-done(((bf16[8,2,4096]{2,1,0:T(2,128)(2,1)}), bf16[8,2,4096]{2,1,0:T(2,128)(2,1)S(1)}, u32[]{:S(2)}, u32[]{:S(2)}) %all-to-all-start.5) | async-done | bytes 131104 | tf_op jit(solution)/shard_map/all_to_all | solution.py:112
  188.1 1.8 fusion.54
  195.8 3.4 %all-to-all-start.2 = ((bf16[8,16,512]{2,1,0:T(8,128)(2,1)}), bf16[8,16,512]{2,1,0:T(8,128)(2,1)S(1)}, u32[]{:S(2)}, u32[]{:S(2)}) async-start(bf16[8,16,512]{2,1,0:T(8,128)(2,1)} %copy.132), calls=%async_computation.2 | async-start | bytes 262144 | tf_op jit(solution)/shard_map/all_to_all | solution.py:143
  199.2 3.1 %add_convert_fusion = bf16[16,4,64,64]{3,2,1,0:T(8,128)(2,1)} fusion(f32[16,4,64,64]{3,2,1,0:T(8,128)} %fusion.54, bf16[8,16,64,1,4]{2,0,4,1,3:T(8,128)(2,1)S(1)} %copy.165, bf16[8,16,64,1,4]{2,0,4,1,3:T(8,128)(2,1)S(1)} %copy.161), kind=kOutput, calls=%fused_computation.20 | convolution fusion | flops 4718592 | bytes 1703936 | tf_op jit(solution)/shard_map/nqcj,nqoj->qjco/dot_general | solution.py:125
  202.7 6.0 %all-to-all-done.2 = bf16[8,16,512]{2,1,0:T(8,128)(2,1)S(1)} async-done(((bf16[8,16,512]{2,1,0:T(8,128)(2,1)}), bf16[8,16,512]{2,1,0:T(8,128)(2,1)S(1)}, u32[]{:S(2)}, u32[]{:S(2)}) %all-to-all-start.2) | async-done | bytes 131104 | tf_op jit(solution)/shard_map/all_to_all | solution.py:143
  212.6 1.9 copy.133
  221.1 11.5 %all-to-all-start.3 = ((bf16[64,2,768]{2,1,0:T(2,128)(2,1)}), bf16[64,2,768]{2,1,0:T(2,128)(2,1)S(1)}, u32[]{:S(2)}, u32[]{:S(2)}) async-start(bf16[64,2,768]{2,1,0:T(2,128)(2,1)} %reshape.363), calls=%async_computation.3 | async-start | bytes 393216 | tf_op jit(solution)/shard_map/all_to_all | solution.py:154
  235.6 7.9 %all-to-all-done.3 = bf16[64,2,768]{2,1,0:T(2,128)(2,1)S(1)} async-done(((bf16[64,2,768]{2,1,0:T(2,128)(2,1)}), bf16[64,2,768]{2,1,0:T(2,128)(2,1)S(1)}, u32[]{:S(2)}, u32[]{:S(2)}) %all-to-all-start.3) | async-done | bytes 196640 | tf_op jit(solution)/shard_map/all_to_all | solution.py:154
  243.8 19.9 %convolution_bitcast_fusion = f32[1,3,64,2304]{3,2,1,0:T(8,128)S(1)} fusion(s32[512]{0:T(512)S(1)} %fusion.84, pred[512]{0:T(512)(128)(4,1)S(1)} %fusion.81, bf16[1,3,64,64,8]{2,4,1,3,0:T(8,128)(2,1)S(1)} %bitcast.196), kind=kOutput, calls=%fused_computation.11 | convolution fusion | flops 468320256 | bytes 1968640 | tf_op jit(solution)/shard_map/dot_general | solution.py:155
  (100 shorter events, 44.0 us)
Async XLA Ops:
  0.6 99.4 %copy-start = (bf16[1,3,64,2304]{3,2,1,0:T(8,128)(2,1)S(1)}, bf16[1,3,64,2304]{3,2,1,0:T(8,128)(2,1)}, u32[]{:S(2)}) copy-start(bf16[1,3,64,2304]{3,2,1,0:T(8,128)(2,1)} %param.9) | copy-start | bytes 2654212
  0.6 6.8 %copy-start.10 = (s32[1,512]{1,0:T(1,128)S(1)}, s32[1,512]{1,0:T(1,128)}, u32[]{:S(2)}) copy-start(s32[1,512]{1,0:T(1,128)} %param.16) | copy-start | bytes 6148
  0.7 6.8 %copy-start.8 = (f32[48,2,64]{2,1,0:T(2,128)S(1)}, f32[48,2,64]{2,1,0:T(2,128)}, u32[]{:S(2)}) copy-start(f32[48,2,64]{2,1,0:T(2,128)} %param.13) | copy-start | bytes 73732
  0.7 7.1 %copy-start.9 = (f32[1,2,512]{2,1,0:T(2,128)S(1)}, f32[1,2,512]{2,1,0:T(2,128)}, u32[]{:S(2)}) copy-start(f32[1,2,512]{2,1,0:T(2,128)} %param.14) | copy-start | bytes 12292
  63.5 19.9 %copy-start.3 = (bf16[3,64,2304]{2,1,0:T(8,128)(2,1)}, bf16[3,64,2304]{2,1,0:T(8,128)(2,1)S(1)}, u32[]{:S(2)}) copy-start(bf16[3,64,2304]{2,1,0:T(8,128)(2,1)S(1)} %copy.121) | copy-start | bytes 2654212
  84.8 37.0 %all-to-all-start = ((bf16[64,2,768]{2,1,0:T(2,128)(2,1)}), bf16[64,2,768]{2,1,0:T(2,128)(2,1)S(1)}, u32[]{:S(2)}, u32[]{:S(2)}) async-start(bf16[64,2,768]{2,1,0:T(2,128)(2,1)} %reshape.359), calls=%async_computation | async-start | bytes 393216 | tf_op jit(solution)/shard_map/all_to_all | solution.py:107
  121.8 24.0 %all-to-all-start.4 = ((bf16[64,2,768]{2,1,0:T(2,128)(2,1)}), bf16[64,2,768]{2,1,0:T(2,128)(2,1)S(1)}, u32[]{:S(2)}, u32[]{:S(2)}) async-start(bf16[64,2,768]{2,1,0:T(2,128)(2,1)} %reshape.365), calls=%async_computation.4 | async-start | bytes 393216 | tf_op jit(solution)/shard_map/all_to_all | solution.py:106
  145.8 18.4 %all-to-all-start.1 = ((bf16[8,2,4096]{2,1,0:T(2,128)(2,1)}), bf16[8,2,4096]{2,1,0:T(2,128)(2,1)S(1)}, u32[]{:S(2)}, u32[]{:S(2)}) async-start(bf16[8,2,4096]{2,1,0:T(2,128)(2,1)} %reshape.361), calls=%async_computation.1 | async-start | bytes 262144 | tf_op jit(solution)/shard_map/all_to_all | solution.py:113
  164.2 16.6 %all-to-all-start.5 = ((bf16[8,2,4096]{2,1,0:T(2,128)(2,1)}), bf16[8,2,4096]{2,1,0:T(2,128)(2,1)S(1)}, u32[]{:S(2)}, u32[]{:S(2)}) async-start(bf16[8,2,4096]{2,1,0:T(2,128)(2,1)} %reshape.367), calls=%async_computation.5 | async-start | bytes 262144 | tf_op jit(solution)/shard_map/all_to_all | solution.py:112
  181.1 8.8 %copy-start.1 = (bf16[16,4,64,128]{3,2,1,0:T(8,128)(2,1)S(1)}, bf16[16,4,64,128]{3,2,1,0:T(8,128)(2,1)}, u32[]{:S(2)}) copy-start(bf16[16,4,64,128]{3,2,1,0:T(8,128)(2,1)} %param.11) | copy-start | bytes 3145732
  188.1 11.1 %copy-start.6 = (bf16[8,16,64,1,4]{2,0,4,1,3:T(8,128)(2,1)}, bf16[8,16,64,1,4]{2,0,4,1,3:T(8,128)(2,1)S(1)}, u32[]{:S(2)}) copy-start(bf16[8,16,64,1,4]{2,0,4,1,3:T(8,128)(2,1)S(1)} %copy.165) | copy-start | bytes 196612
  195.8 13.0 %all-to-all-start.2 = ((bf16[8,16,512]{2,1,0:T(8,128)(2,1)}), bf16[8,16,512]{2,1,0:T(8,128)(2,1)S(1)}, u32[]{:S(2)}, u32[]{:S(2)}) async-start(bf16[8,16,512]{2,1,0:T(8,128)(2,1)} %copy.132), calls=%async_computation.2 | async-start | bytes 262144 | tf_op jit(solution)/shard_map/all_to_all | solution.py:143
  208.8 0.7 copy-start.5
  221.1 22.5 %all-to-all-start.3 = ((bf16[64,2,768]{2,1,0:T(2,128)(2,1)}), bf16[64,2,768]{2,1,0:T(2,128)(2,1)S(1)}, u32[]{:S(2)}, u32[]{:S(2)}) async-start(bf16[64,2,768]{2,1,0:T(2,128)(2,1)} %reshape.363), calls=%async_computation.3 | async-start | bytes 393216 | tf_op jit(solution)/shard_map/all_to_all | solution.py:154
  232.6 1.5 copy-start.2
  243.8 19.9 %copy-start.4 = (bf16[3,64,2304]{2,1,0:T(8,128)(2,1)S(1)}, bf16[3,64,2304]{2,1,0:T(8,128)(2,1)}, u32[]{:S(2)}) copy-start(bf16[3,64,2304]{2,1,0:T(8,128)(2,1)} %copy-done.3) | copy-start | bytes 2654212
  243.8 19.9 %copy-start.7 = (bf16[64,64]{1,0:T(8,128)(2,1)S(1)}, bf16[64,64]{1,0:T(8,128)(2,1)}, u32[]{:S(2)}) copy-start(bf16[64,64]{1,0:T(8,128)(2,1)} %param.12) | copy-start | bytes 24580
where the time goes:
time: 271 us; the launch traced here: 265 us
  matrix products  74.3 us (27%)
  other arithmetic  60 us (22%)
  starting transfers between devices  55.1 us (20%)
  local copies, waits for them, and re-layouts  53.1 us (20%)
  waiting for transfers between devices  20.6 us (8%)
    scatter-add x1, other arithmetic, loss_field(): jnp.zeros(preact.shape, jnp.float32).at[case_idx, row_of, :, col_of]  51.1 us
    dot_general x2, matrix products, lon_forward(): jnp.dot(field.reshape(-1, width), table, preferred_element_type=jnp.float32)  39.5 us
    dot_general x1, matrix products, local(): jnp.dot(synth.reshape(-1, 2 * KX), table.T, preferred_element_type=f32)  19.9 us
    all_to_all x1, starting transfers between devices, local(): lax.all_to_all(loss_spec, 'domain', split_axis=3, concat_axis=1, tiled=True)  15.2 us
    unnamed x38, local copies, waits for them, and re-layouts  14.6 us
    all_to_all x1, starting transfers between devices, local(): lax.all_to_all(synth, 'domain', split_axis=1, concat_axis=3, tiled=True)  11.5 us
    all_to_all x1, starting transfers between devices, local(): lax.all_to_all(input_spec, 'domain', split_axis=3, concat_axis=1, tiled=T...  11.3 us
    another operation x2, local copies, waits for them, and re-layouts  11.2 us
  transfers between devices with their start and end apart: 6, of which 3 were waited for; matrix products, arithmetic and copies ran while one was open for 21% of the time, Pallas kernels for 0%

commit v1 on v0

v1 whole, which is shorter than its diff:
```python
import numpy as np
import ml_dtypes
import jax
import jax.numpy as jnp
from jax import lax
from jax.experimental import pallas as pl
from jax.experimental.pallas import tpu as pltpu
from jax.sharding import PartitionSpec as P

NX = 2304
NY = 2160
KX = 256
KY = 128
STEPS = 48
SLOTS = 512
C = 64
ROWS_DEV = 3
N_DOMAIN = 64
N_DP = 8
ROWS = ROWS_DEV * N_DOMAIN
QL = KY // N_DP
LC = ROWS_DEV * C

two_pi = 6.283185307179586
loss_scale = 8.0
gelu_a = 0.7978845608
gelu_b = 0.044715

f32 = jnp.float32
bf16 = jnp.bfloat16


def lon_table():
    kl, part, kh, block = np.meshgrid(np.arange(2), np.arange(2), np.arange(2), np.arange(N_DOMAIN), indexing="ij")
    wavenum = (4 * block + 2 * kh + kl).reshape(-1, 1).astype(np.int64)
    part = part.reshape(-1, 1)
    phase = (wavenum * np.arange(NX)[None, :] % NX) * (two_pi / NX)
    return np.where(part == 0, np.cos(phase), -np.sin(phase)).astype(ml_dtypes.bfloat16)


def lat_table():
    block, part, ql = np.meshgrid(np.arange(N_DP), np.arange(2), np.arange(QL), indexing="ij")
    part2, l, slab = np.meshgrid(np.arange(2), np.arange(ROWS_DEV), np.arange(N_DOMAIN), indexing="ij")
    index_q = (block * QL + ql).reshape(-1, 1)
    wavenum = np.where(index_q < KY // 2, index_q, NY - KY + index_q).astype(np.int64)
    rows_y = (slab * ROWS_DEV + l).reshape(1, -1) * (NY // ROWS)
    phase = (wavenum * rows_y % NY) * (two_pi / NY)
    part, part2 = part.reshape(-1, 1), part2.reshape(1, -1)
    sine = np.where(part < part2, np.sin(phase), -np.sin(phase))
    return np.where(part == part2, np.cos(phase), sine).astype(ml_dtypes.bfloat16)


def dot(a, b, contract, precision=None):
    return lax.dot_general(a, b, ((contract[0], contract[1]), ((), ())), precision=precision, preferred_element_type=f32)


NN = ((1,), (0,))
NT = ((1,), (1,))
TN = ((0,), (0,))


def slots_kernel(x_ref, p_ref, t_ref, ro_ref, obs_ref, cell_ref, step_ref, cnt_ref, msg_ref, dz_ref, oh_ref, sc_ref):
    cell = cell_ref[...]
    row = (cell >= NX).astype(jnp.int32) + (cell >= 2 * NX).astype(jnp.int32)
    col = cell - row * NX
    for i in range(NX // 256):
        here = lax.broadcasted_iota(jnp.int32, (256, SLOTS), 0) + i * 256
        oh_ref[i * 256 : (i + 1) * 256, :] = (here == col).astype(f32).astype(bf16)
    zall = dot(p_ref[...], oh_ref[...], NN)
    z = jnp.zeros((C, SLOTS), f32)
    for l in range(ROWS_DEV):
        z = z + jnp.where(row == l, zall[l * C : (l + 1) * C], 0.0)
    step_hot = (lax.broadcasted_iota(jnp.int32, (STEPS, SLOTS), 0) == step_ref[...]).astype(f32)
    chosen = dot(ro_ref[...], step_hot, TN, lax.Precision.HIGHEST)
    th = jnp.tanh(gelu_a * (z + gelu_b * (z * z * z)))
    act = 0.5 * z * (1.0 + th)
    slope = 0.5 * (1.0 + th) + 0.5 * z * (1.0 - th * th) * (gelu_a * (1.0 + 3.0 * gelu_b * (z * z)))
    live = (lax.broadcasted_iota(jnp.int32, (1, SLOTS), 1) < cnt_ref[...]).astype(f32)
    back = jnp.zeros((C, SLOTS), f32)
    for j in range(2):
        cj = chosen[j * C : (j + 1) * C]
        velocity = jnp.sum(cj * act, axis=0, keepdims=True)
        back = back + cj * (loss_scale * live * (velocity - obs_ref[j : j + 1, :]))
    dslot = slope * back
    hi = dslot.astype(bf16).astype(f32)
    lo = dslot - hi
    zero = jnp.zeros((C, SLOTS), f32)
    spread = [jnp.where(row == l, part, zero).astype(bf16) for part in (hi, lo) for l in range(ROWS_DEV)]
    both = jnp.concatenate(spread, axis=0)
    step = 768
    for i in range(NX // step):
        grid = dot(both, oh_ref[i * step : (i + 1) * step, :], NT)
        dz_ref[:, i * step : (i + 1) * step] = (grid[:LC] + grid[LC:]).astype(bf16)
    for xz, field in enumerate((x_ref, dz_ref)):
        spec = dot(t_ref[...], field[...], NT)
        for l in range(ROWS_DEV):
            for pk in range(4):
                block = jnp.concatenate(
                    [spec[(kl * 4 + pk) * 64 : (kl * 4 + pk + 1) * 64, l * C : (l + 1) * C] for kl in range(2)], axis=1
                )
                sc_ref[l, pl.ds(xz * 4 + pk, N_DOMAIN, stride=8), :] = block
    for l in range(ROWS_DEV):
        msg_ref[:, :, l * 128 : (l + 1) * 128] = sc_ref[l].reshape(N_DOMAIN, 8, 128).astype(bf16)


def lat_kernel(msg_ref, m_ref, scale_ref, out_ref, sc_ref, rhs_ref):
    for l in range(ROWS_DEV):
        sc_ref[l] = msg_ref[:, :, l * 128 : (l + 1) * 128].astype(f32).reshape(N_DOMAIN * 8, 128)
    for xz in range(2):
        for part in range(2):
            for kh in range(2):
                for l in range(ROWS_DEV):
                    block = sc_ref[l, pl.ds(xz * 4 + part * 2 + kh, N_DOMAIN, stride=8), :]
                    at, lane = (part * ROWS_DEV + l) * N_DOMAIN, (xz * 2 + kh) * 128
                    rhs_ref[at : at + N_DOMAIN, lane : lane + 128] = block.astype(bf16)
    modes = dot(m_ref[...], rhs_ref[...], NN)
    for xz in range(2):
        for kh in range(2):
            b = xz * 2 + kh
            part = modes[:, b * 128 : (b + 1) * 128]
            if xz == 1:
                part = part * scale_ref[:, kh * 128 : (kh + 1) * 128]
            part = part.astype(bf16)
            for d in range(N_DP):
                out_ref[d, b * 32 : (b + 1) * 32, :] = part[d * 32 : (d + 1) * 32]


def load_modes(ref, kh, ql):
    re = ref[pl.ds(kh * 32 + ql, N_DP, stride=64), :]
    im = ref[pl.ds(kh * 32 + QL + ql, N_DP, stride=64), :]
    return re, im


def paired(re, im):
    top = jnp.concatenate([re, im], axis=1)
    low = jnp.concatenate([im, -re], axis=1)
    return jnp.concatenate([top, low], axis=0).astype(bf16)


def mix_kernel(modes_ref, w_ref, out_ref, y_ref, sc_ref):
    for n in range(N_DP):
        y_ref[n * 64 : (n + 1) * 64, :] = modes_ref[n, 64:128, :].astype(f32)
    zero = jnp.zeros((C, C), bf16)
    for kh in range(2):
        for ql in range(QL):
            lhs = paired(*load_modes(y_ref, kh, ql))
            w0, w1 = w_ref[ql, kh * 2], w_ref[ql, kh * 2 + 1]
            rhs = jnp.concatenate(
                [
                    jnp.concatenate([w0[:, :C], zero, w0[:, C:], zero], axis=1),
                    jnp.concatenate([zero, w1[:, :C], zero, w1[:, C:]], axis=1),
                ],
                axis=0,
            )
            back = dot(lhs, rhs, NT)
            sc_ref[pl.ds(kh * 32 + ql, N_DP, stride=64), :] = back[:N_DP]
            sc_ref[pl.ds(kh * 32 + QL + ql, N_DP, stride=64), :] = back[N_DP:]
    for n in range(N_DP):
        out_ref[n] = sc_ref[n * 64 : (n + 1) * 64, :].astype(bf16)


def weight_kernel(modes_ref, out_ref, x_ref, y_ref):
    for n in range(N_DP):
        x_ref[n * 64 : (n + 1) * 64, :] = modes_ref[n, 0:64, :].astype(f32)
        y_ref[n * 64 : (n + 1) * 64, :] = modes_ref[n, 64:128, :].astype(f32)
    for kh in range(2):
        for ql in range(QL):
            rhs = paired(*load_modes(y_ref, kh, ql))
            lhs = jnp.concatenate(load_modes(x_ref, kh, ql), axis=0).astype(bf16)
            grad = dot(lhs, rhs, TN)
            for kl in range(2):
                mine = grad[kl * C : (kl + 1) * C]
                re = mine[:, kl * C : (kl + 1) * C]
                im = mine[:, 128 + kl * C : 128 + (kl + 1) * C]
                out_ref[ql, kh * 2 + kl] = jnp.concatenate([re, im], axis=1).astype(bf16)


def synth_kernel(modes_ref, m_ref, out_ref, d_ref, sc_ref):
    for q in range(N_DP):
        for kh in range(2):
            d_ref[q * 32 : (q + 1) * 32, kh * 128 : (kh + 1) * 128] = modes_ref[q, kh * 32 : (kh + 1) * 32, :]
    lat = dot(m_ref[...], d_ref[...], NN)
    for part in range(2):
        for l in range(ROWS_DEV):
            at = (part * ROWS_DEV + l) * N_DOMAIN
            for kh in range(2):
                block = lat[at : at + N_DOMAIN, kh * 128 : (kh + 1) * 128]
                sc_ref[l, pl.ds(part * 2 + kh, N_DOMAIN, stride=4), :] = block
    for l in range(ROWS_DEV):
        out_ref[:, :, l * 128 : (l + 1) * 128] = sc_ref[l].reshape(N_DOMAIN, 4, 128).astype(bf16)


def grad_kernel(msg_ref, t_ref, dz_ref, pw_ref, out_ref, sc_ref, lhs_ref, pd_ref):
    for l in range(ROWS_DEV):
        sc_ref[l] = msg_ref[:, :, l * 128 : (l + 1) * 128].astype(f32).reshape(N_DOMAIN * 4, 128)
    pd_ref[...] = jnp.zeros((LC, LC), bf16)
    for l in range(ROWS_DEV):
        blocks = [sc_ref[l, pl.ds(pk, N_DOMAIN, stride=4), :] for pk in range(4)]
        turned = jnp.concatenate(blocks, axis=0).T
        for kl in range(2):
            lhs_ref[l * C : (l + 1) * C, kl * 256 : (kl + 1) * 256] = turned[kl * C : (kl + 1) * C].astype(bf16)
        pd_ref[l * C : (l + 1) * C, l * C : (l + 1) * C] = pw_ref[...]
    step = 768
    for i in range(NX // step):
        cols = slice(i * step, (i + 1) * step)
        out = dot(lhs_ref[...], t_ref[:, cols], NN) + dot(pd_ref[...], dz_ref[:, cols], NN)
        out_ref[:, cols] = out.astype(bf16)


def call(kernel, outs, scratch, flops, *args):
    whole = pl.BlockSpec(memory_space=pltpu.VMEM)
    nbytes = sum(a.size * a.dtype.itemsize for a in args)
    return pl.pallas_call(
        kernel,
        out_shape=outs,
        in_specs=[whole] * len(args),
        out_specs=jax.tree.map(lambda _: whole, outs),
        scratch_shapes=scratch,
        cost_estimate=pl.CostEstimate(flops=flops, bytes_accessed=nbytes, transcendentals=0),
        compiler_params=pltpu.CompilerParams(vmem_limit_bytes=40 * 1024 * 1024),
    )(*args)


def local(inputs, preact, spectral_weight, point_weight, readout, observed, cell_index, drift_steps, counts):
    table = jnp.asarray(lon_table())
    lat = lat_table()
    m_fwd, m_inv = jnp.asarray(lat), jnp.asarray(np.ascontiguousarray(lat.T))
    first = (lax.axis_index("domain") == 0) & (jnp.arange(256) < C)
    scale = jnp.where(first, 1.0, 2.0).astype(f32)[None, :] / (NX * ROWS)

    msg, dz = call(
        slots_kernel,
        (
            jax.ShapeDtypeStruct((N_DOMAIN, 8, 384), bf16),
            jax.ShapeDtypeStruct((LC, NX), bf16),
        ),
        [pltpu.VMEM((NX, SLOTS), bf16), pltpu.VMEM((ROWS_DEV, 512, 128), f32)],
        2 * LC * NX * 512 * 5,
        inputs.reshape(LC, NX),
        preact.reshape(LC, NX),
        table,
        readout.reshape(STEPS, 2 * C),
        observed.reshape(2, SLOTS),
        cell_index,
        drift_steps,
        counts,
    )
    msg = lax.all_to_all(msg, "domain", 0, 0, tiled=True)
    modes = call(
        lat_kernel,
        jax.ShapeDtypeStruct((N_DP, 128, 128), bf16),
        [pltpu.VMEM((ROWS_DEV, 512, 128), f32), pltpu.VMEM((384, 512), bf16)],
        2 * 256 * 384 * 512,
        msg,
        m_fwd,
        scale,
    )
    modes = lax.all_to_all(modes, "dp", 0, 0, tiled=True)
    dmodes = call(
        mix_kernel,
        jax.ShapeDtypeStruct((N_DP, 64, 128), bf16),
        [pltpu.VMEM((512, 128), f32), pltpu.VMEM((512, 128), f32)],
        2 * 32 * 128 * 128 * 256,
        modes,
        spectral_weight,
    )
    dmodes = lax.all_to_all(dmodes, "dp", 0, 0, tiled=True)
    weight_grad = call(
        weight_kernel,
        jax.ShapeDtypeStruct((QL, 4, C, 2 * C), bf16),
        [pltpu.VMEM((512, 128), f32), pltpu.VMEM((512, 128), f32)],
        2 * 32 * 128 * 128 * 256,
        modes,
    )
    msg = call(
        synth_kernel,
        jax.ShapeDtypeStruct((N_DOMAIN, 4, 384), bf16),
        [pltpu.VMEM((256, 256), bf16), pltpu.VMEM((ROWS_DEV, 256, 128), f32)],
        2 * 256 * 384 * 256,
        dmodes,
        m_inv,
    )
    msg = lax.all_to_all(msg, "domain", 0, 0, tiled=True)
    input_grad = call(
        grad_kernel,
        jax.ShapeDtypeStruct((LC, NX), bf16),
        [pltpu.VMEM((ROWS_DEV, 256, 128), f32), pltpu.VMEM((LC, 512), bf16), pltpu.VMEM((LC, LC), bf16)],
        2 * LC * NX * 704,
        msg,
        table,
        dz,
        point_weight,
    )
    return (input_grad.reshape(1, ROWS_DEV, C, NX), weight_grad)


def solution(mesh):
    placed = (
        P("dp", "domain", None, None),
        P("dp", "domain", None, None),
        P("dp", "domain", None, None),
        P(),
        P(),
        P("dp", None, "domain"),
        P("dp", "domain"),
        P("dp", "domain"),
        P("dp", "domain"),
    )
    return jax.shard_map(
        local,
        mesh=mesh,
        in_specs=placed,
        out_specs=(P("dp", "domain", None, None), P("dp", "domain", None, None)),
        check_vma=False,
    )
```

time: 271 us -> 98.6 us (0.36); the launches traced: 265 us -> 97.9 us
  matrix products: 74.3 us -> 0 us
  other arithmetic: 60 us -> 0.01 us
  local copies, waits for them, and re-layouts: 53.1 us -> 9.78 us
  starting transfers between devices: 55.1 us -> 20.8 us
  blocking collectives: 0 us -> 30.5 us
  Pallas kernels: 0 us -> 10.2 us
  waiting for transfers between devices: 20.6 us -> 25.3 us
    dot_general x17 -> x0, matrix products: 74.3 us -> none  [the longest x2 39.5 us: lon_forward(): jnp.dot(field.reshape(-1, width), table, preferred_element_type=jnp.float32)]
    scatter-add x1 -> x0, other arithmetic: 51.1 us -> none  [loss_field(): jnp.zeros(preact.shape, jnp.float32).at[case_idx, row_of, :, col_of]]
    all_to_all x6 -> x2, starting transfers between devices: 55.1 us -> 20.8 us  [local(): msg = lax.all_to_all(msg, 'domain', 0, 0, tiled=True)]
    all_to_all x0 -> x2, blocking collectives: none -> 30.5 us  [the longest x1 17.4 us: local(): modes = lax.all_to_all(modes, 'dp', 0, 0, tiled=True)]
    another operation x4 -> x0, local copies, waits for them, and re-layouts: 13.7 us -> none
    pallas_call x0 -> x6, Pallas kernels: none -> 10.2 us  [call(): pl.pallas_call(kernel, out_shape=outs, in_specs=[whole] * len(args), out_...]
    all_to_all x6 -> x0, local copies, waits for them, and re-layouts: 6.04 us -> none  [the longest x2 2.84 us: local(): lax.all_to_all(loss_spec, 'domain', split_axis=3, concat_axis=1, tiled=True)]
    unnamed x38 -> x24, local copies, waits for them, and re-layouts: 14.6 us -> 8.88 us
  transfers between devices with their start and end apart: 6 -> 2, of which waited for: 3 -> 2; matrix products, arithmetic and copies ran while one was open for 21% -> 0% of each run, Pallas kernels for 0% -> 2%
where the time goes in v1:
time: 98.6 us; the launch traced here: 97.9 us
  blocking collectives  30.5 us (31%)
  waiting for transfers between devices  25.3 us (26%)
  starting transfers between devices  20.8 us (21%)
  Pallas kernels  10.2 us (10%)
  local copies, waits for them, and re-layouts  9.78 us (10%)
  between operations  1.36 us (1%)
    all_to_all x2, waiting for transfers between devices, local(): msg = lax.all_to_all(msg, 'domain', 0, 0, tiled=True)  25.3 us
    all_to_all x2, starting transfers between devices, local(): msg = lax.all_to_all(msg, 'domain', 0, 0, tiled=True)  20.8 us
    all_to_all x1, blocking collectives, local(): modes = lax.all_to_all(modes, 'dp', 0, 0, tiled=True)  17.4 us
    all_to_all x1, blocking collectives, local(): dmodes = lax.all_to_all(dmodes, 'dp', 0, 0, tiled=True)  13.1 us
    pallas_call x6, Pallas kernels, call(): pl.pallas_call(kernel, out_shape=outs, in_specs=[whole] * len(args), out_...  10.2 us
    unnamed x24, local copies, waits for them, and re-layouts  8.88 us
  transfers between devices with their start and end apart: 2, of which 2 were waited for; matrix products, arithmetic and copies ran while one was open for 0% of the time, Pallas kernels for 2%

profile of v1, /device:TPU:8, one launch (start us, length us, event | category | flops | bytes accessed | tf_op | source)
XLA Modules:
  0.0 97.9 jit_solution(8716342176533839522)
XLA Ops:
  1.3 0.9 reshape.38.ro_ref
  2.2 1.7 %copy-done = bf16[512,2304]{1,0:T(8,128)(2,1)S(1)} copy-done((bf16[512,2304]{1,0:T(8,128)(2,1)S(1)}, bf16[512,2304]{1,0:T(8,128)(2,1)}, u32[]{:S(2)}) %copy-start) | copy-done | bytes 2359320
  3.8 1.2 %copy-done.7 = bf16[1,3,64,2304]{3,2,1,0:T(8,128)(2,1)S(1)} copy-done((bf16[1,3,64,2304]{3,2,1,0:T(8,128)(2,1)S(1)}, bf16[1,3,64,2304]{3,2,1,0:T(8,128)(2,1)}, u32[]{:S(2)}) %copy-start.7) | copy-done | bytes 884760
  5.0 1.2 %copy-done.8 = bf16[1,3,64,2304]{3,2,1,0:T(8,128)(2,1)S(1)} copy-done((bf16[1,3,64,2304]{3,2,1,0:T(8,128)(2,1)S(1)}, bf16[1,3,64,2304]{3,2,1,0:T(8,128)(2,1)}, u32[]{:S(2)}) %copy-start.8) | copy-done | bytes 884760
  6.2 0.7 copy-done.9
  6.9 0.7 copy-done.10
  7.5 0.7 copy-done.11
  8.2 4.2 %shard_map.131 = (bf16[64,8,384]{2,1,0:T(8,128)(2,1)}, bf16[192,2304]{1,0:T(8,128)(2,1)S(1)}) custom-call(bf16[192,2304]{1,0:T(8,128)(2,1)S(1)} %bitcast.4, bf16[192,2304]{1,0:T(8,128)(2,1)S(1)} %bitcast.5, bf16[512,2304]{1,0:T(8,128)(2,1)S(1)} %copy-done, f32[48,128]{1,0:T(8,128)S(1)} %reshape.38.ro_ref, f32[2,512]{1,0:T(2,128)S(1)} %bitcast.6, ...), custom_call_target="tpu_custom_call" | custom-call | flops 2264924160 | bytes 4161540 | tf_op jit(solution)/shard_map/pallas_call | solution.py:213
  12.4 14.9 %all-to-all-start = ((bf16[64,8,384]{2,1,0:T(8,128)(2,1)}), bf16[64,8,384]{2,1,0:T(8,128)(2,1)S(1)}, u32[]{:S(2)}, u32[]{:S(2)}) async-start(bf16[64,8,384]{2,1,0:T(8,128)(2,1)} %get-tuple-element.4), calls=%async_computation | async-start | bytes 786432 | tf_op jit(solution)/shard_map/all_to_all | solution.py:248
  27.3 15.8 %all-to-all-done.msg_ref = bf16[64,8,384]{2,1,0:T(8,128)(2,1)S(1)} async-done(((bf16[64,8,384]{2,1,0:T(8,128)(2,1)}), bf16[64,8,384]{2,1,0:T(8,128)(2,1)S(1)}, u32[]{:S(2)}, u32[]{:S(2)}) %all-to-all-start) | async-done | bytes 393248 | tf_op jit(solution)/shard_map/all_to_all | solution.py:248
  43.1 0.5 shard_map.132
  43.6 0.0 copy-start.1
  43.6 17.4 %all_to_all.20.modes_ref = bf16[8,128,128]{2,1,0:T(8,128)(2,1)S(1)} all-to-all(bf16[8,128,128]{2,1,0:T(8,128)(2,1)S(1)} %shard_map.132), channel_id=1, replica_groups=mesh['dp'=8,'domain'=64] {'dp'}, dimensions={0} | all-to-all | bytes 524288 | tf_op jit(solution)/shard_map/all_to_all | solution.py:258
  61.0 1.2 %copy-done.2 = bf16[16,4,64,128]{3,2,1,0:T(8,128)(2,1)S(1)} copy-done((bf16[16,4,64,128]{3,2,1,0:T(8,128)(2,1)S(1)}, bf16[16,4,64,128]{3,2,1,0:T(8,128)(2,1)}, u32[]{:S(2)}) %copy-start.2) | copy-done | bytes 1048600
  62.2 0.8 shard_map.133
  62.9 13.1 %all_to_all.21.modes_ref = bf16[8,64,128]{2,1,0:T(8,128)(2,1)S(1)} all-to-all(bf16[8,64,128]{2,1,0:T(8,128)(2,1)S(1)} %shard_map.133), channel_id=1, replica_groups=mesh['dp'=8,'domain'=64] {'dp'}, dimensions={0} | all-to-all | bytes 262144 | tf_op jit(solution)/shard_map/all_to_all | solution.py:267
  76.0 0.9 copy-done.4
  77.0 0.3 shard_map.134
  77.2 0.0 copy-start.3
  77.2 0.7 copy-done.3
  77.9 5.9 %all-to-all-start.3 = ((bf16[64,4,384]{2,1,0:T(4,128)(2,1)}), bf16[64,4,384]{2,1,0:T(4,128)(2,1)}, u32[]{:S(2)}, u32[]{:S(2)}) async-start(bf16[64,4,384]{2,1,0:T(4,128)(2,1)} %copy-done.3), calls=%async_computation.3 | async-start | bytes 393216 | tf_op jit(solution)/shard_map/all_to_all | solution.py:283
  83.8 1.8 %shard_map.136 = bf16[16,4,64,128]{3,2,1,0:T(8,128)(2,1)} custom-call(bf16[8,128,128]{2,1,0:T(8,128)(2,1)S(1)} %all_to_all.20.modes_ref), custom_call_target="tpu_custom_call" | custom-call | flops 268435456 | bytes 262144 | tf_op jit(solution)/shard_map/pallas_call | solution.py:213
  85.6 9.5 %all-to-all-done.3.msg_ref = bf16[64,4,384]{2,1,0:T(4,128)(2,1)} async-done(((bf16[64,4,384]{2,1,0:T(4,128)(2,1)}), bf16[64,4,384]{2,1,0:T(4,128)(2,1)}, u32[]{:S(2)}, u32[]{:S(2)}) %all-to-all-start.3) | async-done | bytes 196640 | tf_op jit(solution)/shard_map/all_to_all | solution.py:283
  95.2 2.7 %shard_map.135 = bf16[192,2304]{1,0:T(8,128)(2,1)} custom-call(bf16[64,4,384]{2,1,0:T(4,128)(2,1)} %all-to-all-done.3.msg_ref, bf16[512,2304]{1,0:T(8,128)(2,1)S(1)} %copy-done.1, bf16[192,2304]{1,0:T(8,128)(2,1)S(1)} %get-tuple-element.5.dz_ref, bf16[64,64]{1,0:T(8,128)(2,1)S(1)} %copy-done.6), custom_call_target="tpu_custom_call" | custom-call | flops 622854144 | bytes 3448832 | tf_op jit(solution)/shard_map/pallas_call | solution.py:213
  (14 shorter events, 0.0 us)
Async XLA Ops:
  2.2 1.7 %copy-start = (bf16[512,2304]{1,0:T(8,128)(2,1)S(1)}, bf16[512,2304]{1,0:T(8,128)(2,1)}, u32[]{:S(2)}) copy-start(bf16[512,2304]{1,0:T(8,128)(2,1)} %constant.21.clone.t_ref) | copy-start | bytes 7077892
  3.8 1.2 %copy-start.7 = (bf16[1,3,64,2304]{3,2,1,0:T(8,128)(2,1)S(1)}, bf16[1,3,64,2304]{3,2,1,0:T(8,128)(2,1)}, u32[]{:S(2)}) copy-start(bf16[1,3,64,2304]{3,2,1,0:T(8,128)(2,1)} %param.12) | copy-start | bytes 2654212
  5.0 1.2 %copy-start.8 = (bf16[1,3,64,2304]{3,2,1,0:T(8,128)(2,1)S(1)}, bf16[1,3,64,2304]{3,2,1,0:T(8,128)(2,1)}, u32[]{:S(2)}) copy-start(bf16[1,3,64,2304]{3,2,1,0:T(8,128)(2,1)} %param.13) | copy-start | bytes 2654212
  6.2 0.7 copy-start.9
  6.9 0.7 copy-start.10
  7.5 0.7 copy-start.11
  8.2 34.9 %copy-start.5 = (bf16[256,384]{1,0:T(8,128)(2,1)S(1)}, bf16[256,384]{1,0:T(8,128)(2,1)}, u32[]{:S(2)}) copy-start(bf16[256,384]{1,0:T(8,128)(2,1)} %constant.22.clone.m_ref) | copy-start | bytes 589828
  12.4 30.7 %all-to-all-start = ((bf16[64,8,384]{2,1,0:T(8,128)(2,1)}), bf16[64,8,384]{2,1,0:T(8,128)(2,1)S(1)}, u32[]{:S(2)}, u32[]{:S(2)}) async-start(bf16[64,8,384]{2,1,0:T(8,128)(2,1)} %get-tuple-element.4), calls=%async_computation | async-start | bytes 786432 | tf_op jit(solution)/shard_map/all_to_all | solution.py:248
  43.1 52.0 %copy-start.6 = (bf16[64,64]{1,0:T(8,128)(2,1)S(1)}, bf16[64,64]{1,0:T(8,128)(2,1)}, u32[]{:S(2)}) copy-start(bf16[64,64]{1,0:T(8,128)(2,1)} %pw_ref.1) | copy-start | bytes 24580
  43.6 51.6 %copy-start.1 = (bf16[512,2304]{1,0:T(8,128)(2,1)S(1)}, bf16[512,2304]{1,0:T(8,128)(2,1)}, u32[]{:S(2)}) copy-start(bf16[512,2304]{1,0:T(8,128)(2,1)} %constant.21.clone.t_ref) | copy-start | bytes 7077892
  60.9 1.2 %copy-start.2 = (bf16[16,4,64,128]{3,2,1,0:T(8,128)(2,1)S(1)}, bf16[16,4,64,128]{3,2,1,0:T(8,128)(2,1)}, u32[]{:S(2)}) copy-start(bf16[16,4,64,128]{3,2,1,0:T(8,128)(2,1)} %w_ref.1) | copy-start | bytes 3145732
  76.0 0.9 copy-start.4
  77.2 0.7 copy-start.3
  77.9 17.2 %all-to-all-start.3 = ((bf16[64,4,384]{2,1,0:T(4,128)(2,1)}), bf16[64,4,384]{2,1,0:T(4,128)(2,1)}, u32[]{:S(2)}, u32[]{:S(2)}) async-start(bf16[64,4,384]{2,1,0:T(4,128)(2,1)} %copy-done.3), calls=%async_computation.3 | async-start | bytes 393216 | tf_op jit(solution)/shard_map/all_to_all | solution.py:283

commit v2 on v1

--- a/solution.py
+++ b/solution.py
@@ -59,26 +59,44 @@
 TN = ((0,), (0,))
 
 
-def slots_kernel(x_ref, p_ref, t_ref, ro_ref, obs_ref, cell_ref, step_ref, cnt_ref, msg_ref, dz_ref, oh_ref, sc_ref):
+def slots_kernel(
+    x_hbm, p_hbm, t_hbm, ro_hbm, obs_hbm, cell_hbm, step_hbm, cnt_ref, msg_hbm, dz_hbm,
+    msg_ref, dz_ref, oh_ref, sc_ref, x_ref, p_ref, t_ref, ro_ref, obs_ref, cell_ref, step_ref, sems, out_sems,
+):
+    moves = (
+        (cell_hbm, cell_ref),
+        (step_hbm, step_ref),
+        (obs_hbm, obs_ref),
+        (ro_hbm, ro_ref),
+        (p_hbm, p_ref),
+        (t_hbm, t_ref),
+        (x_hbm, x_ref),
+    )
+    copies = [pltpu.make_async_copy(src, dst, sems.at[i]) for i, (src, dst) in enumerate(moves)]
+    for copy in copies:
+        copy.start()
+    copies[0].wait()
     cell = cell_ref[...]
     row = (cell >= NX).astype(jnp.int32) + (cell >= 2 * NX).astype(jnp.int32)
     col = cell - row * NX
     for i in range(NX // 256):
         here = lax.broadcasted_iota(jnp.int32, (256, SLOTS), 0) + i * 256
         oh_ref[i * 256 : (i + 1) * 256, :] = (here == col).astype(f32).astype(bf16)
+    for copy in copies[1:5]:
+        copy.wait()
     zall = dot(p_ref[...], oh_ref[...], NN)
     z = jnp.zeros((C, SLOTS), f32)
     for l in range(ROWS_DEV):
         z = z + jnp.where(row == l, zall[l * C : (l + 1) * C], 0.0)
     step_hot = (lax.broadcasted_iota(jnp.int32, (STEPS, SLOTS), 0) == step_ref[...]).astype(f32)
-    chosen = dot(ro_ref[...], step_hot, TN, lax.Precision.HIGHEST)
+    chosen = [dot(ro_ref[:, j, :], step_hot, TN, lax.Precision.HIGHEST) for j in range(2)]
     th = jnp.tanh(gelu_a * (z + gelu_b * (z * z * z)))
     act = 0.5 * z * (1.0 + th)
     slope = 0.5 * (1.0 + th) + 0.5 * z * (1.0 - th * th) * (gelu_a * (1.0 + 3.0 * gelu_b * (z * z)))
-    live = (lax.broadcasted_iota(jnp.int32, (1, SLOTS), 1) < cnt_ref[...]).astype(f32)
+    live = (lax.broadcasted_iota(jnp.int32, (1, SLOTS), 1) < cnt_ref[0, 0]).astype(f32)
     back = jnp.zeros((C, SLOTS), f32)
     for j in range(2):
-        cj = chosen[j * C : (j + 1) * C]
+        cj = chosen[j]
         velocity = jnp.sum(cj * act, axis=0, keepdims=True)
         back = back + cj * (loss_scale * live * (velocity - obs_ref[j : j + 1, :]))
     dslot = slope * back
@@ -88,9 +106,15 @@
     spread = [jnp.where(row == l, part, zero).astype(bf16) for part in (hi, lo) for l in range(ROWS_DEV)]
     both = jnp.concatenate(spread, axis=0)
     step = 768
+    outs = []
     for i in range(NX // step):
         grid = dot(both, oh_ref[i * step : (i + 1) * step, :], NT)
-        dz_ref[:, i * step : (i + 1) * step] = (grid[:LC] + grid[LC:]).astype(bf16)
+        cols = slice(i * step, (i + 1) * step)
+        dz_ref[:, cols] = (grid[:LC] + grid[LC:]).astype(bf16)
+        outs.append(pltpu.make_async_copy(dz_ref.at[:, cols], dz_hbm.at[:, cols], out_sems.at[i]))
+        outs[-1].start()
+    copies[5].wait()
+    copies[6].wait()
     for xz, field in enumerate((x_ref, dz_ref)):
         spec = dot(t_ref[...], field[...], NT)
         for l in range(ROWS_DEV):
@@ -100,10 +124,17 @@
                 )
                 sc_ref[l, pl.ds(xz * 4 + pk, N_DOMAIN, stride=8), :] = block
     for l in range(ROWS_DEV):
-        msg_ref[:, :, l * 128 : (l + 1) * 128] = sc_ref[l].reshape(N_DOMAIN, 8, 128).astype(bf16)
-
-
-def lat_kernel(msg_ref, m_ref, scale_ref, out_ref, sc_ref, rhs_ref):
+        lanes = slice(l * 128, (l + 1) * 128)
+        msg_ref[:, :, lanes] = sc_ref[l].reshape(N_DOMAIN, 8, 128).astype(bf16)
+        outs.append(pltpu.make_async_copy(msg_ref.at[:, :, lanes], msg_hbm.at[:, :, lanes], out_sems.at[3 + l]))
+        outs[-1].start()
+    for copy in outs:
+        copy.wait()
+
+
+def lat_kernel(msg_ref, m_ref, w_ref, out_ref, w_out_ref, m_out_ref, sc_ref, rhs_ref):
+    w_out_ref[...] = w_ref[...]
+    m_out_ref[...] = m_ref[...]
     for l in range(ROWS_DEV):
         sc_ref[l] = msg_ref[:, :, l * 128 : (l + 1) * 128].astype(f32).reshape(N_DOMAIN * 8, 128)
     for xz in range(2):
@@ -113,13 +144,15 @@
                     block = sc_ref[l, pl.ds(xz * 4 + part * 2 + kh, N_DOMAIN, stride=8), :]
                     at, lane = (part * ROWS_DEV + l) * N_DOMAIN, (xz * 2 + kh) * 128
                     rhs_ref[at : at + N_DOMAIN, lane : lane + 128] = block.astype(bf16)
+    lead = (lax.axis_index("domain") == 0) & (lax.broadcasted_iota(jnp.int32, (1, 256), 1) < C)
+    scale = jnp.where(lead, 1.0 / (NX * ROWS), 2.0 / (NX * ROWS))
     modes = dot(m_ref[...], rhs_ref[...], NN)
     for xz in range(2):
         for kh in range(2):
             b = xz * 2 + kh
             part = modes[:, b * 128 : (b + 1) * 128]
             if xz == 1:
-                part = part * scale_ref[:, kh * 128 : (kh + 1) * 128]
+                part = part * scale[:, kh * 128 : (kh + 1) * 128]
             part = part.astype(bf16)
             for d in range(N_DP):
                 out_ref[d, b * 32 : (b + 1) * 32, :] = part[d * 32 : (d + 1) * 32]
@@ -137,7 +170,8 @@
     return jnp.concatenate([top, low], axis=0).astype(bf16)
 
 
-def mix_kernel(modes_ref, w_ref, out_ref, y_ref, sc_ref):
+def mix_kernel(modes_ref, w_ref, m_ref, out_ref, m_out_ref, y_ref, sc_ref):
+    m_out_ref[...] = m_ref[...]
     for n in range(N_DP):
         y_ref[n * 64 : (n + 1) * 64, :] = modes_ref[n, 64:128, :].astype(f32)
     zero = jnp.zeros((C, C), bf16)
@@ -179,7 +213,7 @@
     for q in range(N_DP):
         for kh in range(2):
             d_ref[q * 32 : (q + 1) * 32, kh * 128 : (kh + 1) * 128] = modes_ref[q, kh * 32 : (kh + 1) * 32, :]
-    lat = dot(m_ref[...], d_ref[...], NN)
+    lat = dot(m_ref[...], d_ref[...], TN)
     for part in range(2):
         for l in range(ROWS_DEV):
             at = (part * ROWS_DEV + l) * N_DOMAIN
@@ -190,7 +224,7 @@
         out_ref[:, :, l * 128 : (l + 1) * 128] = sc_ref[l].reshape(N_DOMAIN, 4, 128).astype(bf16)
 
 
-def grad_kernel(msg_ref, t_ref, dz_ref, pw_ref, out_ref, sc_ref, lhs_ref, pd_ref):
+def grad_kernel(msg_ref, t_ref, dz_ref, pw_ref, out_hbm, sc_ref, lhs_ref, pd_ref, out_ref, sems):
     for l in range(ROWS_DEV):
         sc_ref[l] = msg_ref[:, :, l * 128 : (l + 1) * 128].astype(f32).reshape(N_DOMAIN * 4, 128)
     pd_ref[...] = jnp.zeros((LC, LC), bf16)
@@ -201,68 +235,98 @@
             lhs_ref[l * C : (l + 1) * C, kl * 256 : (kl + 1) * 256] = turned[kl * C : (kl + 1) * C].astype(bf16)
         pd_ref[l * C : (l + 1) * C, l * C : (l + 1) * C] = pw_ref[...]
     step = 768
+    copies = []
     for i in range(NX // step):
         cols = slice(i * step, (i + 1) * step)
         out = dot(lhs_ref[...], t_ref[:, cols], NN) + dot(pd_ref[...], dz_ref[:, cols], NN)
         out_ref[:, cols] = out.astype(bf16)
-
-
-def call(kernel, outs, scratch, flops, *args):
-    whole = pl.BlockSpec(memory_space=pltpu.VMEM)
+        copies.append(pltpu.make_async_copy(out_ref.at[:, cols], out_hbm.at[:, cols], sems.at[i]))
+        copies[-1].start()
+    for copy in copies:
+        copy.wait()
+
+
+WHOLE = pl.BlockSpec(memory_space=pltpu.VMEM)
+FAR = pl.BlockSpec(memory_space=pltpu.HBM)
+
+
+def call(kernel, outs, scratch, flops, *args, specs=None, out_specs=None, vmem=40):
     nbytes = sum(a.size * a.dtype.itemsize for a in args)
     return pl.pallas_call(
         kernel,
         out_shape=outs,
-        in_specs=[whole] * len(args),
-        out_specs=jax.tree.map(lambda _: whole, outs),
+        in_specs=specs or [WHOLE] * len(args),
+        out_specs=jax.tree.map(lambda _: WHOLE, outs) if out_specs is None else out_specs,
         scratch_shapes=scratch,
         cost_estimate=pl.CostEstimate(flops=flops, bytes_accessed=nbytes, transcendentals=0),
-        compiler_params=pltpu.CompilerParams(vmem_limit_bytes=40 * 1024 * 1024),
+        compiler_params=pltpu.CompilerParams(vmem_limit_bytes=vmem * 1024 * 1024),
     )(*args)
 
 
-def local(inputs, preact, spectral_weight, point_weight, readout, observed, cell_index, drift_steps, counts):
-    table = jnp.asarray(lon_table())
-    lat = lat_table()
-    m_fwd, m_inv = jnp.asarray(lat), jnp.asarray(np.ascontiguousarray(lat.T))
-    first = (lax.axis_index("domain") == 0) & (jnp.arange(256) < C)
-    scale = jnp.where(first, 1.0, 2.0).astype(f32)[None, :] / (NX * ROWS)
-
-    msg, dz = call(
+def slots_call(inputs, preact, table, readout, observed, cell_index, drift_steps, counts):
+    small = [pltpu.VMEM((1, SLOTS), jnp.int32), pltpu.VMEM((1, SLOTS), jnp.int32)]
+    return call(
         slots_kernel,
         (
             jax.ShapeDtypeStruct((N_DOMAIN, 8, 384), bf16),
             jax.ShapeDtypeStruct((LC, NX), bf16),
         ),
-        [pltpu.VMEM((NX, SLOTS), bf16), pltpu.VMEM((ROWS_DEV, 512, 128), f32)],
+        [
+            pltpu.VMEM((N_DOMAIN, 8, 384), bf16),
+            pltpu.VMEM((LC, NX), bf16),
+            pltpu.VMEM((NX, SLOTS), bf16),
+            pltpu.VMEM((ROWS_DEV, 512, 128), f32),
+            pltpu.VMEM((LC, NX), bf16),
+            pltpu.VMEM((LC, NX), bf16),
+            pltpu.VMEM((512, NX), bf16),
+            pltpu.VMEM((STEPS, 2, C), f32),
+            pltpu.VMEM((2, SLOTS), f32),
+            *small,
+            pltpu.SemaphoreType.DMA((7,)),
+            pltpu.SemaphoreType.DMA((6,)),
+        ],
         2 * LC * NX * 512 * 5,
         inputs.reshape(LC, NX),
         preact.reshape(LC, NX),
         table,
-        readout.reshape(STEPS, 2 * C),
+        readout,
         observed.reshape(2, SLOTS),
         cell_index,
         drift_steps,
         counts,
-    )
+        specs=[FAR] * 7 + [pl.BlockSpec(memory_space=pltpu.SMEM)],
+        out_specs=(FAR, FAR),
+        vmem=59,
+    )
+
+
+def local(inputs, preact, spectral_weight, point_weight, readout, observed, cell_index, drift_steps, counts):
+    table = jnp.asarray(lon_table())
+    lat = jnp.asarray(lat_table())
+    msg, dz = slots_call(inputs, preact, table, readout, observed, cell_index, drift_steps, counts)
     msg = lax.all_to_all(msg, "domain", 0, 0, tiled=True)
-    modes = call(
+    modes, weight, lat = call(
         lat_kernel,
-        jax.ShapeDtypeStruct((N_DP, 128, 128), bf16),
+        (
+            jax.ShapeDtypeStruct((N_DP, 128, 128), bf16),
+            jax.ShapeDtypeStruct((QL, 4, C, 2 * C), bf16),
+            jax.ShapeDtypeStruct(lat.shape, bf16),
+        ),
         [pltpu.VMEM((ROWS_DEV, 512, 128), f32), pltpu.VMEM((384, 512), bf16)],
         2 * 256 * 384 * 512,
         msg,
-        m_fwd,
-        scale,
+        lat,
+        spectral_weight,
     )
     modes = lax.all_to_all(modes, "dp", 0, 0, tiled=True)
-    dmodes = call(
+    dmodes, lat = call(
         mix_kernel,
-        jax.ShapeDtypeStruct((N_DP, 64, 128), bf16),
+        (jax.ShapeDtypeStruct((N_DP, 64, 128), bf16), jax.ShapeDtypeStruct(lat.shape, bf16)),
         [pltpu.VMEM((512, 128), f32), pltpu.VMEM((512, 128), f32)],
         2 * 32 * 128 * 128 * 256,
         modes,
-        spectral_weight,
+        weight,
+        lat,
     )
     dmodes = lax.all_to_all(dmodes, "dp", 0, 0, tiled=True)
     weight_grad = call(
@@ -275,21 +339,31 @@
     msg = call(
         synth_kernel,
         jax.ShapeDtypeStruct((N_DOMAIN, 4, 384), bf16),
-        [pltpu.VMEM((256, 256), bf16), pltpu.VMEM((ROWS_DEV, 256, 128), f32)],
+        [
+            pltpu.VMEM((256, 256), bf16),
+            pltpu.VMEM((ROWS_DEV, 256, 128), f32),
+        ],
         2 * 256 * 384 * 256,
         dmodes,
-        m_inv,
+        lat,
     )
     msg = lax.all_to_all(msg, "domain", 0, 0, tiled=True)
     input_grad = call(
         grad_kernel,
         jax.ShapeDtypeStruct((LC, NX), bf16),
-        [pltpu.VMEM((ROWS_DEV, 256, 128), f32), pltpu.VMEM((LC, 512), bf16), pltpu.VMEM((LC, LC), bf16)],
+        [
+            pltpu.VMEM((ROWS_DEV, 256, 128), f32),
+            pltpu.VMEM((LC, 512), bf16),
+            pltpu.VMEM((LC, LC), bf16),
+            pltpu.VMEM((LC, NX), bf16),
+            pltpu.SemaphoreType.DMA((3,)),
+        ],
         2 * LC * NX * 704,
         msg,
         table,
         dz,
         point_weight,
+        out_specs=FAR,
     )
     return (input_grad.reshape(1, ROWS_DEV, C, NX), weight_grad)
 

time: 98.6 us -> 90.8 us (0.921)
  blocking collectives: 30.5 us -> 61.3 us
  waiting for transfers between devices: 25.3 us -> 9.5 us
  starting transfers between devices: 20.8 us -> 5.88 us
  local copies, waits for them, and re-layouts: 9.78 us -> 0.7 us
  Pallas kernels: 10.2 us -> 11.8 us
    all_to_all x0 -> x1, blocking collectives: none -> 30.7 us  [local(): msg = lax.all_to_all(msg, 'domain', 0, 0, tiled=True)]
    all_to_all x2 -> x1, waiting for transfers between devices: 25.3 us -> 9.5 us  [local(): msg = lax.all_to_all(msg, 'domain', 0, 0, tiled=True)]
    all_to_all x2 -> x1, starting transfers between devices: 20.8 us -> 5.88 us  [local(): msg = lax.all_to_all(msg, 'domain', 0, 0, tiled=True)]
    unnamed x24 -> x12, local copies, waits for them, and re-layouts: 8.88 us -> 0.7 us
    pallas_call x6, Pallas kernels: 10.2 us -> 11.8 us  [call(): pl.pallas_call(kernel, out_shape=outs, in_specs=specs or [WHOLE] * len(ar...]
  transfers between devices with their start and end apart: 2 -> 1, of which waited for: 2 -> 1; matrix products, arithmetic and copies ran while one was open for 0% -> 0% of each run, Pallas kernels for 2% -> 2%
where the time goes in v2:
time: 90.8 us; the launch traced here: 90.5 us
  blocking collectives  61.3 us (68%)
  Pallas kernels  11.8 us (13%)
  waiting for transfers between devices  9.5 us (10%)
  starting transfers between devices  5.88 us (6%)
  between operations  1.37 us (2%)
    all_to_all x1, blocking collectives, local(): msg = lax.all_to_all(msg, 'domain', 0, 0, tiled=True)  30.7 us
    all_to_all x1, blocking collectives, local(): modes = lax.all_to_all(modes, 'dp', 0, 0, tiled=True)  17.5 us
    all_to_all x1, blocking collectives, local(): dmodes = lax.all_to_all(dmodes, 'dp', 0, 0, tiled=True)  13.1 us
    pallas_call x6, Pallas kernels, call(): pl.pallas_call(kernel, out_shape=outs, in_specs=specs or [WHOLE] * len(ar...  11.8 us
    all_to_all x1, waiting for transfers between devices, local(): msg = lax.all_to_all(msg, 'domain', 0, 0, tiled=True)  9.5 us
    all_to_all x1, starting transfers between devices, local(): msg = lax.all_to_all(msg, 'domain', 0, 0, tiled=True)  5.88 us
  transfers between devices with their start and end apart: 1, of which 1 were waited for; matrix products, arithmetic and copies ran while one was open for 0% of the time, Pallas kernels for 2%

profile of v2, /device:TPU:8, one launch (start us, length us, event | category | flops | bytes accessed | tf_op | source)
XLA Modules:
  0.0 90.5 jit_solution(12828884802431137034)
XLA Ops:
  1.3 0.0 copy-start.1
  1.3 0.0 copy-start.4
  1.3 5.7 %shard_map.122 = (bf16[64,8,384]{2,1,0:T(8,128)(2,1)}, bf16[192,2304]{1,0:T(8,128)(2,1)}) custom-call(bf16[192,2304]{1,0:T(8,128)(2,1)} %bitcast.5, bf16[192,2304]{1,0:T(8,128)(2,1)} %bitcast.6, bf16[512,2304]{1,0:T(8,128)(2,1)} %constant.4.clone.t_hbm.t_ref, f32[48,2,64]{2,1,0:T(2,128)} %ro_hbm.1, f32[2,512]{1,0:T(2,128)} %bitcast.7, s32[1,512]{1,0:T(1,128)} %cell_hbm.1, ...), custom_call_target="tpu_custom_call" | custom-call | flops 2264924160 | bytes 4161540 | tf_op jit(solution)/shard_map/pallas_call | solution.py:255
  7.0 30.7 %all_to_all.20.msg_ref = bf16[64,8,384]{2,1,0:T(8,128)(2,1)S(1)} all-to-all(bf16[64,8,384]{2,1,0:T(8,128)(2,1)} %get-tuple-element.9), channel_id=1, replica_groups=mesh['dp'=8,'domain'=64] {'domain'}, dimensions={0} | all-to-all | bytes 786432 | tf_op jit(solution)/shard_map/all_to_all | solution.py:307
  37.7 0.0 copy-done.1
  37.7 0.0 copy-done.4
  37.7 0.5 shard_map.123
  38.2 0.0 copy-start
  38.2 0.0 copy-start.2
  38.3 0.0 copy-start.5
  38.3 17.5 %all_to_all.21.modes_ref = bf16[8,128,128]{2,1,0:T(8,128)(2,1)S(1)} all-to-all(bf16[8,128,128]{2,1,0:T(8,128)(2,1)S(1)} %get-tuple-element.10), channel_id=1, replica_groups=mesh['dp'=8,'domain'=64] {'dp'}, dimensions={0} | all-to-all | bytes 524288 | tf_op jit(solution)/shard_map/all_to_all | solution.py:321
  55.8 0.8 shard_map.124
  56.5 13.1 %all_to_all.22.modes_ref = bf16[8,64,128]{2,1,0:T(8,128)(2,1)S(1)} all-to-all(bf16[8,64,128]{2,1,0:T(8,128)(2,1)S(1)} %get-tuple-element.13), channel_id=1, replica_groups=mesh['dp'=8,'domain'=64] {'dp'}, dimensions={0} | all-to-all | bytes 262144 | tf_op jit(solution)/shard_map/all_to_all | solution.py:331
  69.6 0.3 shard_map.125
  69.9 0.0 copy-start.3
  69.9 0.7 copy-done.3
  70.6 5.9 %all-to-all-start.3 = ((bf16[64,4,384]{2,1,0:T(4,128)(2,1)}), bf16[64,4,384]{2,1,0:T(4,128)(2,1)}, u32[]{:S(2)}, u32[]{:S(2)}) async-start(bf16[64,4,384]{2,1,0:T(4,128)(2,1)} %copy-done.3), calls=%async_computation.3 | async-start | bytes 393216 | tf_op jit(solution)/shard_map/all_to_all | solution.py:350
  76.5 1.8 %shard_map.127 = bf16[16,4,64,128]{3,2,1,0:T(8,128)(2,1)} custom-call(bf16[8,128,128]{2,1,0:T(8,128)(2,1)S(1)} %all_to_all.21.modes_ref), custom_call_target="tpu_custom_call" | custom-call | flops 268435456 | bytes 262144 | tf_op jit(solution)/shard_map/pallas_call | solution.py:255
  78.3 9.5 %all-to-all-done.3.msg_ref = bf16[64,4,384]{2,1,0:T(4,128)(2,1)} async-done(((bf16[64,4,384]{2,1,0:T(4,128)(2,1)}), bf16[64,4,384]{2,1,0:T(4,128)(2,1)}, u32[]{:S(2)}, u32[]{:S(2)}) %all-to-all-start.3) | async-done | bytes 196640 | tf_op jit(solution)/shard_map/all_to_all | solution.py:350
  87.8 0.0 copy-done
  87.8 0.0 copy-done.2
  87.8 0.0 copy-done.5
  87.8 2.7 %shard_map.126 = bf16[192,2304]{1,0:T(8,128)(2,1)} custom-call(bf16[64,4,384]{2,1,0:T(4,128)(2,1)} %all-to-all-done.3.msg_ref, bf16[512,2304]{1,0:T(8,128)(2,1)S(1)} %copy-done, bf16[192,2304]{1,0:T(8,128)(2,1)S(1)} %copy-done.2, bf16[64,64]{1,0:T(8,128)(2,1)S(1)} %copy-done.5), custom_call_target="tpu_custom_call" | custom-call | flops 622854144 | bytes 3448832 | tf_op jit(solution)/shard_map/pallas_call | solution.py:255
Async XLA Ops:
  1.3 36.4 %copy-start.1 = (bf16[16,4,64,128]{3,2,1,0:T(8,128)(2,1)S(1)}, bf16[16,4,64,128]{3,2,1,0:T(8,128)(2,1)}, u32[]{:S(2)}) copy-start(bf16[16,4,64,128]{3,2,1,0:T(8,128)(2,1)} %w_ref.1) | copy-start | bytes 3145732
  1.3 36.4 %copy-start.4 = (bf16[256,384]{1,0:T(8,128)(2,1)S(1)}, bf16[256,384]{1,0:T(8,128)(2,1)}, u32[]{:S(2)}) copy-start(bf16[256,384]{1,0:T(8,128)(2,1)} %constant.5.clone.m_ref) | copy-start | bytes 589828
  38.2 49.6 %copy-start = (bf16[512,2304]{1,0:T(8,128)(2,1)S(1)}, bf16[512,2304]{1,0:T(8,128)(2,1)}, u32[]{:S(2)}) copy-start(bf16[512,2304]{1,0:T(8,128)(2,1)} %constant.4.clone.t_hbm.t_ref) | copy-start | bytes 7077892
  38.2 49.6 %copy-start.2 = (bf16[192,2304]{1,0:T(8,128)(2,1)S(1)}, bf16[192,2304]{1,0:T(8,128)(2,1)}, u32[]{:S(2)}) copy-start(bf16[192,2304]{1,0:T(8,128)(2,1)} %get-tuple-element.15.dz_ref) | copy-start | bytes 2654212
  38.3 49.6 %copy-start.5 = (bf16[64,64]{1,0:T(8,128)(2,1)S(1)}, bf16[64,64]{1,0:T(8,128)(2,1)}, u32[]{:S(2)}) copy-start(bf16[64,64]{1,0:T(8,128)(2,1)} %pw_ref.1) | copy-start | bytes 24580
  69.9 0.7 copy-start.3
  70.6 17.2 %all-to-all-start.3 = ((bf16[64,4,384]{2,1,0:T(4,128)(2,1)}), bf16[64,4,384]{2,1,0:T(4,128)(2,1)}, u32[]{:S(2)}, u32[]{:S(2)}) async-start(bf16[64,4,384]{2,1,0:T(4,128)(2,1)} %copy-done.3), calls=%async_computation.3 | async-start | bytes 393216 | tf_op jit(solution)/shard_map/all_to_all | solution.py:350

commit v3 on v2

--- a/solution.py
+++ b/solution.py
@@ -20,6 +20,7 @@
 ROWS = ROWS_DEV * N_DOMAIN
 QL = KY // N_DP
 LC = ROWS_DEV * C
+HALF = NX // 2
 
 two_pi = 6.283185307179586
 loss_scale = 8.0
@@ -34,7 +35,7 @@
     kl, part, kh, block = np.meshgrid(np.arange(2), np.arange(2), np.arange(2), np.arange(N_DOMAIN), indexing="ij")
     wavenum = (4 * block + 2 * kh + kl).reshape(-1, 1).astype(np.int64)
     part = part.reshape(-1, 1)
-    phase = (wavenum * np.arange(NX)[None, :] % NX) * (two_pi / NX)
+    phase = (wavenum * np.arange(HALF)[None, :] % NX) * (two_pi / NX)
     return np.where(part == 0, np.cos(phase), -np.sin(phase)).astype(ml_dtypes.bfloat16)
 
 
@@ -59,16 +60,40 @@
 TN = ((0,), (0,))
 
 
+def where_slots(cell_ref):
+    cell = cell_ref[...]
+    row = (cell >= NX).astype(jnp.int32) + (cell >= 2 * NX).astype(jnp.int32)
+    return row, cell - row * NX
+
+
+def hot_slots(col, oh_ref):
+    step = 128
+    for i in range(oh_ref.shape[0] // step):
+        here = lax.broadcasted_iota(jnp.int32, (step, SLOTS), 0) + i * step
+        oh_ref[i * step : (i + 1) * step, :] = (here == col).astype(f32).astype(bf16)
+
+
+def spread_slots(row, dslot):
+    hi = dslot.astype(bf16).astype(f32)
+    lo = dslot - hi
+    zero = jnp.zeros((C, SLOTS), f32)
+    return [
+        jnp.concatenate([jnp.where(row == l, part, zero).astype(bf16) for l in range(ROWS_DEV)], axis=0)
+        for part in (hi, lo)
+    ]
+
+
 def slots_kernel(
-    x_hbm, p_hbm, t_hbm, ro_hbm, obs_hbm, cell_hbm, step_hbm, cnt_ref, msg_hbm, dz_hbm,
-    msg_ref, dz_ref, oh_ref, sc_ref, x_ref, p_ref, t_ref, ro_ref, obs_ref, cell_ref, step_ref, sems, out_sems,
+    x_hbm, p_hbm, t_hbm, ro_hbm, obs_hbm, cell_hbm, step_hbm, cnt_ref, msg_hbm, dslot_hbm,
+    msg_ref, dslot_ref, oh_ref, sc_ref, x_ref, p_ref, t_ref, ro_ref, obs_ref, cell_ref, step_ref, sems, out_sems,
 ):
     moves = (
         (cell_hbm, cell_ref),
         (step_hbm, step_ref),
         (obs_hbm, obs_ref),
         (ro_hbm, ro_ref),
-        (p_hbm, p_ref),
+        (p_hbm.at[:, :HALF], p_ref.at[:LC]),
+        (p_hbm.at[:, HALF:], p_ref.at[LC:]),
         (t_hbm, t_ref),
         (x_hbm, x_ref),
     )
@@ -76,18 +101,20 @@
     for copy in copies:
         copy.start()
     copies[0].wait()
-    cell = cell_ref[...]
-    row = (cell >= NX).astype(jnp.int32) + (cell >= 2 * NX).astype(jnp.int32)
-    col = cell - row * NX
-    for i in range(NX // 256):
-        here = lax.broadcasted_iota(jnp.int32, (256, SLOTS), 0) + i * 256
-        oh_ref[i * 256 : (i + 1) * 256, :] = (here == col).astype(f32).astype(bf16)
-    for copy in copies[1:5]:
+    row, col = where_slots(cell_ref)
+    east = (col >= HALF).astype(jnp.int32)
+    hot_slots(col - east * HALF, oh_ref)
+    place = east * ROWS_DEV + row
+    for copy in copies[1:6]:
         copy.wait()
     zall = dot(p_ref[...], oh_ref[...], NN)
     z = jnp.zeros((C, SLOTS), f32)
-    for l in range(ROWS_DEV):
-        z = z + jnp.where(row == l, zall[l * C : (l + 1) * C], 0.0)
+    for i in range(2 * ROWS_DEV):
+        z = z + jnp.where(place == i, zall[i * C : (i + 1) * C], 0.0)
+    copies[6].wait()
+    west = dot(t_ref[:256], oh_ref[...], NN).astype(bf16)
+    turn = (1 - 2 * east).astype(f32)
+    rest = (dot(t_ref[256:], oh_ref[...], NN) * turn).astype(bf16)
     step_hot = (lax.broadcasted_iota(jnp.int32, (STEPS, SLOTS), 0) == step_ref[...]).astype(f32)
     chosen = [dot(ro_ref[:, j, :], step_hot, TN, lax.Precision.HIGHEST) for j in range(2)]
     th = jnp.tanh(gelu_a * (z + gelu_b * (z * z * z)))
@@ -100,36 +127,42 @@
         velocity = jnp.sum(cj * act, axis=0, keepdims=True)
         back = back + cj * (loss_scale * live * (velocity - obs_ref[j : j + 1, :]))
     dslot = slope * back
-    hi = dslot.astype(bf16).astype(f32)
-    lo = dslot - hi
-    zero = jnp.zeros((C, SLOTS), f32)
-    spread = [jnp.where(row == l, part, zero).astype(bf16) for part in (hi, lo) for l in range(ROWS_DEV)]
-    both = jnp.concatenate(spread, axis=0)
-    step = 768
-    outs = []
-    for i in range(NX // step):
-        grid = dot(both, oh_ref[i * step : (i + 1) * step, :], NT)
-        cols = slice(i * step, (i + 1) * step)
-        dz_ref[:, cols] = (grid[:LC] + grid[LC:]).astype(bf16)
-        outs.append(pltpu.make_async_copy(dz_ref.at[:, cols], dz_hbm.at[:, cols], out_sems.at[i]))
-        outs[-1].start()
-    copies[5].wait()
-    copies[6].wait()
-    for xz, field in enumerate((x_ref, dz_ref)):
-        spec = dot(t_ref[...], field[...], NT)
+    dslot_ref[...] = dslot
+    outs = [pltpu.make_async_copy(dslot_ref, dslot_hbm, out_sems.at[3])]
+    outs[0].start()
+
+    def place_spectra(xz, even, odd):
         for l in range(ROWS_DEV):
             for pk in range(4):
                 block = jnp.concatenate(
-                    [spec[(kl * 4 + pk) * 64 : (kl * 4 + pk + 1) * 64, l * C : (l + 1) * C] for kl in range(2)], axis=1
+                    [spec[pk * 64 : (pk + 1) * 64, l * C : (l + 1) * C] for spec in (even, odd)], axis=1
                 )
                 sc_ref[l, pl.ds(xz * 4 + pk, N_DOMAIN, stride=8), :] = block
+
+    hi, lo = spread_slots(row, dslot)
+    place_spectra(1, dot(west, hi, NT) + dot(west, lo, NT), dot(rest, hi, NT) + dot(rest, lo, NT))
+    copies[7].wait()
+    near, far = x_ref[:, :HALF].astype(f32), x_ref[:, HALF:].astype(f32)
+    place_spectra(
+        0, dot(t_ref[:256], (near + far).astype(bf16), NT), dot(t_ref[256:], (near - far).astype(bf16), NT)
+    )
     for l in range(ROWS_DEV):
         lanes = slice(l * 128, (l + 1) * 128)
         msg_ref[:, :, lanes] = sc_ref[l].reshape(N_DOMAIN, 8, 128).astype(bf16)
-        outs.append(pltpu.make_async_copy(msg_ref.at[:, :, lanes], msg_hbm.at[:, :, lanes], out_sems.at[3 + l]))
+        outs.append(pltpu.make_async_copy(msg_ref.at[:, :, lanes], msg_hbm.at[:, :, lanes], out_sems.at[l]))
         outs[-1].start()
     for copy in outs:
         copy.wait()
+
+
+def scatter_kernel(dslot_ref, cell_ref, dz_ref, oh_ref):
+    row, col = where_slots(cell_ref)
+    hot_slots(col, oh_ref)
+    both = jnp.concatenate(spread_slots(row, dslot_ref[...]), axis=0)
+    step = 768
+    for i in range(NX // step):
+        grid = dot(both, oh_ref[i * step : (i + 1) * step, :], NT)
+        dz_ref[:, i * step : (i + 1) * step] = (grid[:LC] + grid[LC:]).astype(bf16)
 
 
 def lat_kernel(msg_ref, m_ref, w_ref, out_ref, w_out_ref, m_out_ref, sc_ref, rhs_ref):
@@ -234,14 +267,17 @@
         for kl in range(2):
             lhs_ref[l * C : (l + 1) * C, kl * 256 : (kl + 1) * 256] = turned[kl * C : (kl + 1) * C].astype(bf16)
         pd_ref[l * C : (l + 1) * C, l * C : (l + 1) * C] = pw_ref[...]
-    step = 768
+    step = 384
     copies = []
-    for i in range(NX // step):
+    for i in range(HALF // step):
         cols = slice(i * step, (i + 1) * step)
-        out = dot(lhs_ref[...], t_ref[:, cols], NN) + dot(pd_ref[...], dz_ref[:, cols], NN)
-        out_ref[:, cols] = out.astype(bf16)
-        copies.append(pltpu.make_async_copy(out_ref.at[:, cols], out_hbm.at[:, cols], sems.at[i]))
-        copies[-1].start()
+        even = dot(lhs_ref[:, :256], t_ref[:256, cols], NN)
+        odd = dot(lhs_ref[:, 256:], t_ref[256:, cols], NN)
+        for h, spec in enumerate((even + odd, even - odd)):
+            cols = slice(h * HALF + i * step, h * HALF + (i + 1) * step)
+            out_ref[:, cols] = (spec + dot(pd_ref[...], dz_ref[:, cols], NN)).astype(bf16)
+            copies.append(pltpu.make_async_copy(out_ref.at[:, cols], out_hbm.at[:, cols], sems.at[2 * i + h]))
+            copies[-1].start()
     for copy in copies:
         copy.wait()
 
@@ -269,23 +305,23 @@
         slots_kernel,
         (
             jax.ShapeDtypeStruct((N_DOMAIN, 8, 384), bf16),
-            jax.ShapeDtypeStruct((LC, NX), bf16),
+            jax.ShapeDtypeStruct((C, SLOTS), f32),
         ),
         [
             pltpu.VMEM((N_DOMAIN, 8, 384), bf16),
-            pltpu.VMEM((LC, NX), bf16),
-            pltpu.VMEM((NX, SLOTS), bf16),
+            pltpu.VMEM((C, SLOTS), f32),
+            pltpu.VMEM((HALF, SLOTS), bf16),
             pltpu.VMEM((ROWS_DEV, 512, 128), f32),
             pltpu.VMEM((LC, NX), bf16),
-            pltpu.VMEM((LC, NX), bf16),
-            pltpu.VMEM((512, NX), bf16),
+            pltpu.VMEM((2 * LC, HALF), bf16),
+            pltpu.VMEM((512, HALF), bf16),
             pltpu.VMEM((STEPS, 2, C), f32),
             pltpu.VMEM((2, SLOTS), f32),
             *small,
-            pltpu.SemaphoreType.DMA((7,)),
-            pltpu.SemaphoreType.DMA((6,)),
+            pltpu.SemaphoreType.DMA((8,)),
+            pltpu.SemaphoreType.DMA((4,)),
         ],
-        2 * LC * NX * 512 * 5,
+        2 * LC * NX * 512 * 4,
         inputs.reshape(LC, NX),
         preact.reshape(LC, NX),
         table,
@@ -303,7 +339,7 @@
 def local(inputs, preact, spectral_weight, point_weight, readout, observed, cell_index, drift_steps, counts):
     table = jnp.asarray(lon_table())
     lat = jnp.asarray(lat_table())
-    msg, dz = slots_call(inputs, preact, table, readout, observed, cell_index, drift_steps, counts)
+    msg, dslot = slots_call(inputs, preact, table, readout, observed, cell_index, drift_steps, counts)
     msg = lax.all_to_all(msg, "domain", 0, 0, tiled=True)
     modes, weight, lat = call(
         lat_kernel,
@@ -336,6 +372,14 @@
         2 * 32 * 128 * 128 * 256,
         modes,
     )
+    dz = call(
+        scatter_kernel,
+        jax.ShapeDtypeStruct((LC, NX), bf16),
+        [pltpu.VMEM((NX, SLOTS), bf16)],
+        2 * LC * NX * 512 * 2,
+        dslot,
+        cell_index,
+    )
     msg = call(
         synth_kernel,
         jax.ShapeDtypeStruct((N_DOMAIN, 4, 384), bf16),
@@ -356,9 +400,9 @@
             pltpu.VMEM((LC, 512), bf16),
             pltpu.VMEM((LC, LC), bf16),
             pltpu.VMEM((LC, NX), bf16),
-            pltpu.SemaphoreType.DMA((3,)),
+            pltpu.SemaphoreType.DMA((6,)),
         ],
-        2 * LC * NX * 704,
+        2 * LC * NX * 448,
         msg,
         table,
         dz,

time: 90.8 us -> 88.2 us (0.971)
  waiting for transfers between devices: 9.5 us -> 8.38 us
    all_to_all x1, waiting for transfers between devices: 9.5 us -> 8.38 us  [local(): msg = lax.all_to_all(msg, 'domain', 0, 0, tiled=True)]
    pallas_call x6 -> x7, Pallas kernels: 11.8 us -> 11.9 us  [call(): pl.pallas_call(kernel, out_shape=outs, in_specs=specs or [WHOLE] * len(ar...]
  transfers between devices with their start and end apart: 1 -> 1, of which waited for: 1 -> 1; matrix products, arithmetic and copies ran while one was open for 0% -> 0% of each run, Pallas kernels for 2% -> 3%
where the time goes in v3:
time: 88.2 us; the launch traced here: 87.9 us
  blocking collectives  61 us (69%)
  Pallas kernels  11.9 us (13%)
  waiting for transfers between devices  8.38 us (10%)
  starting transfers between devices  5.13 us (6%)
  between operations  1.37 us (2%)
    all_to_all x1, blocking collectives, local(): msg = lax.all_to_all(msg, 'domain', 0, 0, tiled=True)  30.7 us
    all_to_all x1, blocking collectives, local(): modes = lax.all_to_all(modes, 'dp', 0, 0, tiled=True)  17.2 us
    all_to_all x1, blocking collectives, local(): dmodes = lax.all_to_all(dmodes, 'dp', 0, 0, tiled=True)  13.1 us
    pallas_call x7, Pallas kernels, call(): pl.pallas_call(kernel, out_shape=outs, in_specs=specs or [WHOLE] * len(ar...  11.9 us
    all_to_all x1, waiting for transfers between devices, local(): msg = lax.all_to_all(msg, 'domain', 0, 0, tiled=True)  8.38 us
    all_to_all x1, starting transfers between devices, local(): msg = lax.all_to_all(msg, 'domain', 0, 0, tiled=True)  5.13 us
  transfers between devices with their start and end apart: 1, of which 1 were waited for; matrix products, arithmetic and copies ran while one was open for 0% of the time, Pallas kernels for 3%

profile of v3, /device:TPU:8, one launch (start us, length us, event | category | flops | bytes accessed | tf_op | source)
XLA Modules:
  0.0 87.9 jit_solution(8794007470960435293)
XLA Ops:
  1.3 0.0 copy-start.1
  1.3 0.0 copy-start.2
  1.3 5.1 %shard_map.122 = (bf16[64,8,384]{2,1,0:T(8,128)(2,1)}, f32[64,512]{1,0:T(8,128)}) custom-call(bf16[192,2304]{1,0:T(8,128)(2,1)} %bitcast.5, bf16[192,2304]{1,0:T(8,128)(2,1)} %bitcast.6, bf16[512,1152]{1,0:T(8,128)(2,1)} %constant.4.clone.t_hbm.t_ref, f32[48,2,64]{2,1,0:T(2,128)} %ro_hbm.1, f32[2,512]{1,0:T(2,128)} %bitcast.7, s32[1,512]{1,0:T(1,128)} %cell_ref.1, ...), custom_call_target="tpu_custom_call" | custom-call | flops 1811939328 | bytes 2981892 | tf_op jit(solution)/shard_map/pallas_call | solution.py:291
  6.4 30.7 %all_to_all.20.msg_ref = bf16[64,8,384]{2,1,0:T(8,128)(2,1)S(1)} all-to-all(bf16[64,8,384]{2,1,0:T(8,128)(2,1)} %get-tuple-element.9), channel_id=1, replica_groups=mesh['dp'=8,'domain'=64] {'domain'}, dimensions={0} | all-to-all | bytes 786432 | tf_op jit(solution)/shard_map/all_to_all | solution.py:343
  37.1 0.0 copy-done.1
  37.1 0.0 copy-done.2
  37.1 0.5 shard_map.123
  37.7 17.2 %all_to_all.21.modes_ref = bf16[8,128,128]{2,1,0:T(8,128)(2,1)S(1)} all-to-all(bf16[8,128,128]{2,1,0:T(8,128)(2,1)S(1)} %get-tuple-element.10), channel_id=1, replica_groups=mesh['dp'=8,'domain'=64] {'dp'}, dimensions={0} | all-to-all | bytes 524288 | tf_op jit(solution)/shard_map/all_to_all | solution.py:357
  54.9 0.0 copy-start.4
  54.9 0.0 copy-start.5
  54.9 0.8 shard_map.124
  55.7 13.1 %all_to_all.22.modes_ref = bf16[8,64,128]{2,1,0:T(8,128)(2,1)S(1)} all-to-all(bf16[8,64,128]{2,1,0:T(8,128)(2,1)S(1)} %get-tuple-element.13), channel_id=1, replica_groups=mesh['dp'=8,'domain'=64] {'dp'}, dimensions={0} | all-to-all | bytes 262144 | tf_op jit(solution)/shard_map/all_to_all | solution.py:367
  68.8 1.0 %shard_map.125 = bf16[64,4,384]{2,1,0:T(4,128)(2,1)} custom-call(bf16[8,64,128]{2,1,0:T(8,128)(2,1)S(1)} %all_to_all.22.modes_ref, bf16[256,384]{1,0:T(8,128)(2,1)S(1)} %get-tuple-element.14.m_ref), custom_call_target="tpu_custom_call" | custom-call | flops 50331648 | bytes 327680 | tf_op jit(solution)/shard_map/pallas_call | solution.py:291
  69.7 5.1 %all-to-all-start.3 = ((bf16[64,4,384]{2,1,0:T(4,128)(2,1)}), bf16[64,4,384]{2,1,0:T(4,128)(2,1)S(1)}, u32[]{:S(2)}, u32[]{:S(2)}) async-start(bf16[64,4,384]{2,1,0:T(4,128)(2,1)} %shard_map.125), calls=%async_computation.3 | async-start | bytes 393216 | tf_op jit(solution)/shard_map/all_to_all | solution.py:394
  74.9 0.0 copy-done.4
  74.9 0.0 copy-done.5
  74.9 1.1 %shard_map.126.dz_ref = bf16[192,2304]{1,0:T(8,128)(2,1)S(1)} custom-call(f32[64,512]{1,0:T(8,128)S(1)} %copy-done.5, s32[1,512]{1,0:T(1,128)S(1)} %copy-done.4), custom_call_target="tpu_custom_call" | custom-call | flops 905969664 | bytes 133120 | tf_op jit(solution)/shard_map/pallas_call | solution.py:291
  76.0 0.0 copy-start
  76.1 0.0 copy-start.3
  76.1 1.8 %shard_map.128 = bf16[16,4,64,128]{3,2,1,0:T(8,128)(2,1)} custom-call(bf16[8,128,128]{2,1,0:T(8,128)(2,1)S(1)} %all_to_all.21.modes_ref), custom_call_target="tpu_custom_call" | custom-call | flops 268435456 | bytes 262144 | tf_op jit(solution)/shard_map/pallas_call | solution.py:291
  77.9 8.4 %all-to-all-done.3.msg_ref = bf16[64,4,384]{2,1,0:T(4,128)(2,1)S(1)} async-done(((bf16[64,4,384]{2,1,0:T(4,128)(2,1)}), bf16[64,4,384]{2,1,0:T(4,128)(2,1)S(1)}, u32[]{:S(2)}, u32[]{:S(2)}) %all-to-all-start.3) | async-done | bytes 196640 | tf_op jit(solution)/shard_map/all_to_all | solution.py:394
  86.3 0.0 copy-done
  86.3 0.0 copy-done.3
  86.3 1.6 %shard_map.127 = bf16[192,2304]{1,0:T(8,128)(2,1)} custom-call(bf16[64,4,384]{2,1,0:T(4,128)(2,1)S(1)} %all-to-all-done.3.msg_ref, bf16[512,1152]{1,0:T(8,128)(2,1)S(1)} %copy-done, bf16[192,2304]{1,0:T(8,128)(2,1)S(1)} %shard_map.126.dz_ref, bf16[64,64]{1,0:T(8,128)(2,1)S(1)} %copy-done.3), custom_call_target="tpu_custom_call" | custom-call | flops 396361728 | bytes 2269184 | tf_op jit(solution)/shard_map/pallas_call | solution.py:291
Async XLA Ops:
  1.3 35.9 %copy-start.1 = (bf16[16,4,64,128]{3,2,1,0:T(8,128)(2,1)S(1)}, bf16[16,4,64,128]{3,2,1,0:T(8,128)(2,1)}, u32[]{:S(2)}) copy-start(bf16[16,4,64,128]{3,2,1,0:T(8,128)(2,1)} %w_ref.1) | copy-start | bytes 3145732
  1.3 35.9 %copy-start.2 = (bf16[256,384]{1,0:T(8,128)(2,1)S(1)}, bf16[256,384]{1,0:T(8,128)(2,1)}, u32[]{:S(2)}) copy-start(bf16[256,384]{1,0:T(8,128)(2,1)} %constant.5.clone.m_ref) | copy-start | bytes 589828
  54.9 20.0 %copy-start.4 = (s32[1,512]{1,0:T(1,128)S(1)}, s32[1,512]{1,0:T(1,128)}, u32[]{:S(2)}) copy-start(s32[1,512]{1,0:T(1,128)} %cell_ref.1) | copy-start | bytes 6148
  54.9 20.0 %copy-start.5 = (f32[64,512]{1,0:T(8,128)S(1)}, f32[64,512]{1,0:T(8,128)}, u32[]{:S(2)}) copy-start(f32[64,512]{1,0:T(8,128)} %get-tuple-element.15.dslot_ref) | copy-start | bytes 393220
  69.7 16.5 %all-to-all-start.3 = ((bf16[64,4,384]{2,1,0:T(4,128)(2,1)}), bf16[64,4,384]{2,1,0:T(4,128)(2,1)S(1)}, u32[]{:S(2)}, u32[]{:S(2)}) async-start(bf16[64,4,384]{2,1,0:T(4,128)(2,1)} %shard_map.125), calls=%async_computation.3 | async-start | bytes 393216 | tf_op jit(solution)/shard_map/all_to_all | solution.py:394
  76.0 10.3 %copy-start = (bf16[512,1152]{1,0:T(8,128)(2,1)S(1)}, bf16[512,1152]{1,0:T(8,128)(2,1)}, u32[]{:S(2)}) copy-start(bf16[512,1152]{1,0:T(8,128)(2,1)} %constant.4.clone.t_hbm.t_ref) | copy-start | bytes 3538948
  76.1 10.2 %copy-start.3 = (bf16[64,64]{1,0:T(8,128)(2,1)S(1)}, bf16[64,64]{1,0:T(8,128)(2,1)}, u32[]{:S(2)}) copy-start(bf16[64,64]{1,0:T(8,128)(2,1)} %pw_ref.1) | copy-start | bytes 24580

commit v4 on v3

--- a/solution.py
+++ b/solution.py
@@ -84,8 +84,7 @@
 
 
 def slots_kernel(
-    x_hbm, p_hbm, t_hbm, ro_hbm, obs_hbm, cell_hbm, step_hbm, cnt_ref, msg_hbm, dslot_hbm,
-    msg_ref, dslot_ref, oh_ref, sc_ref, x_ref, p_ref, t_ref, ro_ref, obs_ref, cell_ref, step_ref, sems, out_sems,
+    x_hbm, p_hbm, t_hbm, ro_hbm, obs_hbm, cell_hbm, step_hbm, cnt_ref, msg_ref, dslot_ref, oh_ref, sc_ref, x_ref, p_ref, t_ref, ro_ref, obs_ref, cell_ref, step_ref, sems,
 ):
     moves = (
         (cell_hbm, cell_ref),
@@ -105,7 +104,18 @@
     east = (col >= HALF).astype(jnp.int32)
     hot_slots(col - east * HALF, oh_ref)
     place = east * ROWS_DEV + row
-    for copy in copies[1:6]:
+    for copy in copies[1:4]:
+        copy.wait()
+    step_hot = (lax.broadcasted_iota(jnp.int32, (STEPS, SLOTS), 0) == step_ref[...]).astype(f32).astype(bf16)
+    step_hot = jnp.concatenate([step_hot] * 3, axis=0)
+    chosen = []
+    for j in range(2):
+        full = ro_ref[:, j, :]
+        top = full.astype(bf16)
+        mid = (full - top.astype(f32)).astype(bf16)
+        low = (full - top.astype(f32) - mid.astype(f32)).astype(bf16)
+        chosen.append(dot(jnp.concatenate([top, mid, low], axis=0), step_hot, TN))
+    for copy in copies[4:6]:
         copy.wait()
     zall = dot(p_ref[...], oh_ref[...], NN)
     z = jnp.zeros((C, SLOTS), f32)
@@ -115,8 +125,6 @@
     west = dot(t_ref[:256], oh_ref[...], NN).astype(bf16)
     turn = (1 - 2 * east).astype(f32)
     rest = (dot(t_ref[256:], oh_ref[...], NN) * turn).astype(bf16)
-    step_hot = (lax.broadcasted_iota(jnp.int32, (STEPS, SLOTS), 0) == step_ref[...]).astype(f32)
-    chosen = [dot(ro_ref[:, j, :], step_hot, TN, lax.Precision.HIGHEST) for j in range(2)]
     th = jnp.tanh(gelu_a * (z + gelu_b * (z * z * z)))
     act = 0.5 * z * (1.0 + th)
     slope = 0.5 * (1.0 + th) + 0.5 * z * (1.0 - th * th) * (gelu_a * (1.0 + 3.0 * gelu_b * (z * z)))
@@ -128,8 +136,6 @@
         back = back + cj * (loss_scale * live * (velocity - obs_ref[j : j + 1, :]))
     dslot = slope * back
     dslot_ref[...] = dslot
-    outs = [pltpu.make_async_copy(dslot_ref, dslot_hbm, out_sems.at[3])]
-    outs[0].start()
 
     def place_spectra(xz, even, odd):
         for l in range(ROWS_DEV):
@@ -139,20 +145,17 @@
                 )
                 sc_ref[l, pl.ds(xz * 4 + pk, N_DOMAIN, stride=8), :] = block
 
-    hi, lo = spread_slots(row, dslot)
-    place_spectra(1, dot(west, hi, NT) + dot(west, lo, NT), dot(rest, hi, NT) + dot(rest, lo, NT))
     copies[7].wait()
     near, far = x_ref[:, :HALF].astype(f32), x_ref[:, HALF:].astype(f32)
     place_spectra(
         0, dot(t_ref[:256], (near + far).astype(bf16), NT), dot(t_ref[256:], (near - far).astype(bf16), NT)
     )
+    hi, lo = spread_slots(row, dslot)
+    both = jnp.concatenate([hi, lo], axis=0)
+    parts = [dot(waves, both, NT) for waves in (west, rest)]
+    place_spectra(1, *[spec[:, :LC] + spec[:, LC:] for spec in parts])
     for l in range(ROWS_DEV):
-        lanes = slice(l * 128, (l + 1) * 128)
-        msg_ref[:, :, lanes] = sc_ref[l].reshape(N_DOMAIN, 8, 128).astype(bf16)
-        outs.append(pltpu.make_async_copy(msg_ref.at[:, :, lanes], msg_hbm.at[:, :, lanes], out_sems.at[l]))
-        outs[-1].start()
-    for copy in outs:
-        copy.wait()
+        msg_ref[:, :, l * 128 : (l + 1) * 128] = sc_ref[l].reshape(N_DOMAIN, 8, 128).astype(bf16)
 
 
 def scatter_kernel(dslot_ref, cell_ref, dz_ref, oh_ref):
@@ -165,9 +168,8 @@
         dz_ref[:, i * step : (i + 1) * step] = (grid[:LC] + grid[LC:]).astype(bf16)
 
 
-def lat_kernel(msg_ref, m_ref, w_ref, out_ref, w_out_ref, m_out_ref, sc_ref, rhs_ref):
-    w_out_ref[...] = w_ref[...]
-    m_out_ref[...] = m_ref[...]
+def lat_kernel(msg_ref, m_ref, w_ref, out_ref, sc_ref, rhs_ref):
+    del w_ref
     for l in range(ROWS_DEV):
         sc_ref[l] = msg_ref[:, :, l * 128 : (l + 1) * 128].astype(f32).reshape(N_DOMAIN * 8, 128)
     for xz in range(2):
@@ -308,8 +310,6 @@
             jax.ShapeDtypeStruct((C, SLOTS), f32),
         ),
         [
-            pltpu.VMEM((N_DOMAIN, 8, 384), bf16),
-            pltpu.VMEM((C, SLOTS), f32),
             pltpu.VMEM((HALF, SLOTS), bf16),
             pltpu.VMEM((ROWS_DEV, 512, 128), f32),
             pltpu.VMEM((LC, NX), bf16),
@@ -319,20 +319,22 @@
             pltpu.VMEM((2, SLOTS), f32),
             *small,
             pltpu.SemaphoreType.DMA((8,)),
-            pltpu.SemaphoreType.DMA((4,)),
         ],
         2 * LC * NX * 512 * 4,
-        inputs.reshape(LC, NX),
-        preact.reshape(LC, NX),
-        table,
-        readout,
-        observed.reshape(2, SLOTS),
-        cell_index,
-        drift_steps,
+        *[
+            pltpu.with_memory_space_constraint(array, pltpu.HBM)
+            for array in (
+                inputs.reshape(LC, NX),
+                preact.reshape(LC, NX),
+                table,
+                readout,
+                observed.reshape(2, SLOTS),
+                cell_index,
+                drift_steps,
+            )
+        ],
         counts,
         specs=[FAR] * 7 + [pl.BlockSpec(memory_space=pltpu.SMEM)],
-        out_specs=(FAR, FAR),
-        vmem=59,
     )
 
 
@@ -341,13 +343,9 @@
     lat = jnp.asarray(lat_table())
     msg, dslot = slots_call(inputs, preact, table, readout, observed, cell_index, drift_steps, counts)
     msg = lax.all_to_all(msg, "domain", 0, 0, tiled=True)
-    modes, weight, lat = call(
+    modes = call(
         lat_kernel,
-        (
-            jax.ShapeDtypeStruct((N_DP, 128, 128), bf16),
-            jax.ShapeDtypeStruct((QL, 4, C, 2 * C), bf16),
-            jax.ShapeDtypeStruct(lat.shape, bf16),
-        ),
+        jax.ShapeDtypeStruct((N_DP, 128, 128), bf16),
         [pltpu.VMEM((ROWS_DEV, 512, 128), f32), pltpu.VMEM((384, 512), bf16)],
         2 * 256 * 384 * 512,
         msg,
@@ -361,7 +359,7 @@
         [pltpu.VMEM((512, 128), f32), pltpu.VMEM((512, 128), f32)],
         2 * 32 * 128 * 128 * 256,
         modes,
-        weight,
+        spectral_weight,
         lat,
     )
     dmodes = lax.all_to_all(dmodes, "dp", 0, 0, tiled=True)

time: 88.2 us -> 86.8 us (0.984)
  Pallas kernels: 11.9 us -> 10.7 us
    pallas_call x7, Pallas kernels: 11.9 us -> 10.7 us  [call(): pl.pallas_call(kernel, out_shape=outs, in_specs=specs or [WHOLE] * len(ar...]
where the time goes in v4:
time: 86.8 us; the launch traced here: 86.5 us
  blocking collectives  60.8 us (70%)
  Pallas kernels  10.7 us (12%)
  waiting for transfers between devices  8.39 us (10%)
  starting transfers between devices  5.13 us (6%)
  between operations  1.36 us (2%)
    all_to_all x1, blocking collectives, local(): msg = lax.all_to_all(msg, 'domain', 0, 0, tiled=True)  30.5 us
    all_to_all x1, blocking collectives, local(): modes = lax.all_to_all(modes, 'dp', 0, 0, tiled=True)  17.2 us
    all_to_all x1, blocking collectives, local(): dmodes = lax.all_to_all(dmodes, 'dp', 0, 0, tiled=True)  13.1 us
    pallas_call x7, Pallas kernels, call(): pl.pallas_call(kernel, out_shape=outs, in_specs=specs or [WHOLE] * len(ar...  10.7 us
    all_to_all x1, waiting for transfers between devices, local(): msg = lax.all_to_all(msg, 'domain', 0, 0, tiled=True)  8.39 us
    all_to_all x1, starting transfers between devices, local(): msg = lax.all_to_all(msg, 'domain', 0, 0, tiled=True)  5.13 us
  transfers between devices with their start and end apart: 1, of which 1 were waited for; matrix products, arithmetic and copies ran while one was open for 0% of the time, Pallas kernels for 3%

profile of v4, /device:TPU:8, one launch (start us, length us, event | category | flops | bytes accessed | tf_op | source)
XLA Modules:
  0.0 86.5 jit_solution(7691891419873993910)
XLA Ops:
  1.3 0.0 copy-start
  1.3 0.0 copy-start.2
  1.3 4.0 %shard_map.122 = (bf16[64,8,384]{2,1,0:T(8,128)(2,1)S(1)}, f32[64,512]{1,0:T(8,128)S(1)}) custom-call(bf16[192,2304]{1,0:T(8,128)(2,1)} %bitcast.5, bf16[192,2304]{1,0:T(8,128)(2,1)} %bitcast.6, bf16[512,1152]{1,0:T(8,128)(2,1)} %constant.4.clone.t_hbm.t_ref, f32[48,2,64]{2,1,0:T(2,128)} %ro_hbm.1, f32[2,512]{1,0:T(2,128)} %bitcast.7, s32[1,512]{1,0:T(1,128)} %cell_ref.1, ...), custom_call_target="tpu_custom_call" | custom-call | flops 1811939328 | bytes 2981892 | tf_op jit(solution)/shard_map/pallas_call | solution.py:293
  5.3 30.5 %all_to_all.20.msg_ref = bf16[64,8,384]{2,1,0:T(8,128)(2,1)S(1)} all-to-all(bf16[64,8,384]{2,1,0:T(8,128)(2,1)S(1)} %get-tuple-element.6), channel_id=1, replica_groups=mesh['dp'=8,'domain'=64] {'domain'}, dimensions={0} | all-to-all | bytes 786432 | tf_op jit(solution)/shard_map/all_to_all | solution.py:345
  35.8 0.0 copy-done
  35.8 0.0 copy-done.2
  35.8 0.5 shard_map.123
  36.3 17.2 %all_to_all.21.modes_ref = bf16[8,128,128]{2,1,0:T(8,128)(2,1)S(1)} all-to-all(bf16[8,128,128]{2,1,0:T(8,128)(2,1)S(1)} %shard_map.123), channel_id=1, replica_groups=mesh['dp'=8,'domain'=64] {'dp'}, dimensions={0} | all-to-all | bytes 524288 | tf_op jit(solution)/shard_map/all_to_all | solution.py:355
  53.5 0.0 copy-start.4
  53.5 0.8 shard_map.124
  54.3 13.1 %all_to_all.22.modes_ref = bf16[8,64,128]{2,1,0:T(8,128)(2,1)S(1)} all-to-all(bf16[8,64,128]{2,1,0:T(8,128)(2,1)S(1)} %get-tuple-element.7), channel_id=1, replica_groups=mesh['dp'=8,'domain'=64] {'dp'}, dimensions={0} | all-to-all | bytes 262144 | tf_op jit(solution)/shard_map/all_to_all | solution.py:365
  67.4 1.0 %shard_map.125 = bf16[64,4,384]{2,1,0:T(4,128)(2,1)} custom-call(bf16[8,64,128]{2,1,0:T(8,128)(2,1)S(1)} %all_to_all.22.modes_ref, bf16[256,384]{1,0:T(8,128)(2,1)S(1)} %get-tuple-element.8.m_ref), custom_call_target="tpu_custom_call" | custom-call | flops 50331648 | bytes 327680 | tf_op jit(solution)/shard_map/pallas_call | solution.py:293
  68.3 5.1 %all-to-all-start.3 = ((bf16[64,4,384]{2,1,0:T(4,128)(2,1)}), bf16[64,4,384]{2,1,0:T(4,128)(2,1)S(1)}, u32[]{:S(2)}, u32[]{:S(2)}) async-start(bf16[64,4,384]{2,1,0:T(4,128)(2,1)} %shard_map.125), calls=%async_computation.3 | async-start | bytes 393216 | tf_op jit(solution)/shard_map/all_to_all | solution.py:392
  73.5 0.0 copy-done.4
  73.5 1.1 %shard_map.126.dz_ref = bf16[192,2304]{1,0:T(8,128)(2,1)S(1)} custom-call(f32[64,512]{1,0:T(8,128)S(1)} %get-tuple-element.9.dslot_ref, s32[1,512]{1,0:T(1,128)S(1)} %copy-done.4), custom_call_target="tpu_custom_call" | custom-call | flops 905969664 | bytes 133120 | tf_op jit(solution)/shard_map/pallas_call | solution.py:293
  74.6 0.0 copy-start.1
  74.6 0.0 copy-start.3
  74.6 1.8 %shard_map.128 = bf16[16,4,64,128]{3,2,1,0:T(8,128)(2,1)} custom-call(bf16[8,128,128]{2,1,0:T(8,128)(2,1)S(1)} %all_to_all.21.modes_ref), custom_call_target="tpu_custom_call" | custom-call | flops 268435456 | bytes 262144 | tf_op jit(solution)/shard_map/pallas_call | solution.py:293
  76.5 8.4 %all-to-all-done.3.msg_ref = bf16[64,4,384]{2,1,0:T(4,128)(2,1)S(1)} async-done(((bf16[64,4,384]{2,1,0:T(4,128)(2,1)}), bf16[64,4,384]{2,1,0:T(4,128)(2,1)S(1)}, u32[]{:S(2)}, u32[]{:S(2)}) %all-to-all-start.3) | async-done | bytes 196640 | tf_op jit(solution)/shard_map/all_to_all | solution.py:392
  84.9 0.0 copy-done.1
  84.9 0.0 copy-done.3
  84.9 1.6 %shard_map.127 = bf16[192,2304]{1,0:T(8,128)(2,1)} custom-call(bf16[64,4,384]{2,1,0:T(4,128)(2,1)S(1)} %all-to-all-done.3.msg_ref, bf16[512,1152]{1,0:T(8,128)(2,1)S(1)} %copy-done.1, bf16[192,2304]{1,0:T(8,128)(2,1)S(1)} %shard_map.126.dz_ref, bf16[64,64]{1,0:T(8,128)(2,1)S(1)} %copy-done.3), custom_call_target="tpu_custom_call" | custom-call | flops 396361728 | bytes 2269184 | tf_op jit(solution)/shard_map/pallas_call | solution.py:293
Async XLA Ops:
  1.3 34.5 %copy-start = (bf16[16,4,64,128]{3,2,1,0:T(8,128)(2,1)S(1)}, bf16[16,4,64,128]{3,2,1,0:T(8,128)(2,1)}, u32[]{:S(2)}) copy-start(bf16[16,4,64,128]{3,2,1,0:T(8,128)(2,1)} %w_ref.3) | copy-start | bytes 3145732
  1.3 34.5 %copy-start.2 = (bf16[256,384]{1,0:T(8,128)(2,1)S(1)}, bf16[256,384]{1,0:T(8,128)(2,1)}, u32[]{:S(2)}) copy-start(bf16[256,384]{1,0:T(8,128)(2,1)} %constant.5.clone.m_ref) | copy-start | bytes 589828
  53.5 20.0 %copy-start.4 = (s32[1,512]{1,0:T(1,128)S(1)}, s32[1,512]{1,0:T(1,128)}, u32[]{:S(2)}) copy-start(s32[1,512]{1,0:T(1,128)} %cell_ref.1) | copy-start | bytes 6148
  68.3 16.5 %all-to-all-start.3 = ((bf16[64,4,384]{2,1,0:T(4,128)(2,1)}), bf16[64,4,384]{2,1,0:T(4,128)(2,1)S(1)}, u32[]{:S(2)}, u32[]{:S(2)}) async-start(bf16[64,4,384]{2,1,0:T(4,128)(2,1)} %shard_map.125), calls=%async_computation.3 | async-start | bytes 393216 | tf_op jit(solution)/shard_map/all_to_all | solution.py:392
  74.6 10.3 %copy-start.1 = (bf16[512,1152]{1,0:T(8,128)(2,1)S(1)}, bf16[512,1152]{1,0:T(8,128)(2,1)}, u32[]{:S(2)}) copy-start(bf16[512,1152]{1,0:T(8,128)(2,1)} %constant.4.clone.t_hbm.t_ref) | copy-start | bytes 3538948
  74.6 10.3 %copy-start.3 = (bf16[64,64]{1,0:T(8,128)(2,1)S(1)}, bf16[64,64]{1,0:T(8,128)(2,1)}, u32[]{:S(2)}) copy-start(bf16[64,64]{1,0:T(8,128)(2,1)} %pw_ref.1) | copy-start | bytes 24580

commit v5 on v4

--- a/solution.py
+++ b/solution.py
@@ -21,6 +21,7 @@
 QL = KY // N_DP
 LC = ROWS_DEV * C
 HALF = NX // 2
+EDGES = (0, 640, 1152)
 
 two_pi = 6.283185307179586
 loss_scale = 8.0
@@ -73,6 +74,31 @@
         oh_ref[i * step : (i + 1) * step, :] = (here == col).astype(f32).astype(bf16)
 
 
+def turn(steps):
+    steps = steps - NX * jnp.floor(steps * (1.0 / NX) + 0.5)
+    quarter = jnp.floor(steps * (4.0 / NX) + 0.5)
+    a = (steps - (NX // 4) * quarter) * (two_pi / NX)
+    b = a * a
+    cosine = 1.0 + b * (-1 / 2 + b * (1 / 24 + b * (-1 / 720 + b * (1 / 40320))))
+    sine = a * (1.0 + b * (-1 / 6 + b * (1 / 120 + b * (-1 / 5040 + b * (1 / 362880)))))
+    odd = jnp.abs(quarter) == 1.0
+    cosine, sine = jnp.where(odd, sine, cosine), jnp.where(odd, cosine, sine)
+    cosine = jnp.where((quarter == 1.0) | (jnp.abs(quarter) == 2.0), -cosine, cosine)
+    return cosine, jnp.where((quarter < 0.0) | (quarter == 2.0), -sine, sine)
+
+
+def slot_waves(col, out_ref):
+    x = col.astype(f32)
+    block = lax.broadcasted_iota(jnp.int32, (N_DOMAIN, SLOTS), 0).astype(f32)
+    cos4, sin4 = turn(4.0 * block * x)
+    for kl in range(2):
+        for kh in range(2):
+            cosj, sinj = turn((2.0 * kh + kl) * x)
+            at = kl * 256 + kh * 64
+            out_ref[at : at + 64, :] = (cos4 * cosj - sin4 * sinj).astype(bf16)
+            out_ref[at + 128 : at + 192, :] = (-sin4 * cosj - cos4 * sinj).astype(bf16)
+
+
 def spread_slots(row, dslot):
     hi = dslot.astype(bf16).astype(f32)
     lo = dslot - hi
@@ -84,7 +110,7 @@
 
 
 def slots_kernel(
-    x_hbm, p_hbm, t_hbm, ro_hbm, obs_hbm, cell_hbm, step_hbm, cnt_ref, msg_ref, dslot_ref, oh_ref, sc_ref, x_ref, p_ref, t_ref, ro_ref, obs_ref, cell_ref, step_ref, sems,
+    x_hbm, p_hbm, t_hbm, ro_hbm, obs_hbm, cell_hbm, step_hbm, cnt_ref, msg_ref, dslot_ref, oh_ref, wave_ref, sc_ref, x_ref, p_ref, t_ref, ro_ref, obs_ref, cell_ref, step_ref, sems,
 ):
     moves = (
         (cell_hbm, cell_ref),
@@ -103,6 +129,7 @@
     row, col = where_slots(cell_ref)
     east = (col >= HALF).astype(jnp.int32)
     hot_slots(col - east * HALF, oh_ref)
+    slot_waves(col, wave_ref)
     place = east * ROWS_DEV + row
     for copy in copies[1:4]:
         copy.wait()
@@ -121,10 +148,6 @@
     z = jnp.zeros((C, SLOTS), f32)
     for i in range(2 * ROWS_DEV):
         z = z + jnp.where(place == i, zall[i * C : (i + 1) * C], 0.0)
-    copies[6].wait()
-    west = dot(t_ref[:256], oh_ref[...], NN).astype(bf16)
-    turn = (1 - 2 * east).astype(f32)
-    rest = (dot(t_ref[256:], oh_ref[...], NN) * turn).astype(bf16)
     th = jnp.tanh(gelu_a * (z + gelu_b * (z * z * z)))
     act = 0.5 * z * (1.0 + th)
     slope = 0.5 * (1.0 + th) + 0.5 * z * (1.0 - th * th) * (gelu_a * (1.0 + 3.0 * gelu_b * (z * z)))
@@ -145,6 +168,7 @@
                 )
                 sc_ref[l, pl.ds(xz * 4 + pk, N_DOMAIN, stride=8), :] = block
 
+    copies[6].wait()
     copies[7].wait()
     near, far = x_ref[:, :HALF].astype(f32), x_ref[:, HALF:].astype(f32)
     place_spectra(
@@ -152,7 +176,7 @@
     )
     hi, lo = spread_slots(row, dslot)
     both = jnp.concatenate([hi, lo], axis=0)
-    parts = [dot(waves, both, NT) for waves in (west, rest)]
+    parts = [dot(waves, both, NT) for waves in (wave_ref[:256], wave_ref[256:])]
     place_spectra(1, *[spec[:, :LC] + spec[:, LC:] for spec in parts])
     for l in range(ROWS_DEV):
         msg_ref[:, :, l * 128 : (l + 1) * 128] = sc_ref[l].reshape(N_DOMAIN, 8, 128).astype(bf16)
@@ -269,16 +293,15 @@
         for kl in range(2):
             lhs_ref[l * C : (l + 1) * C, kl * 256 : (kl + 1) * 256] = turned[kl * C : (kl + 1) * C].astype(bf16)
         pd_ref[l * C : (l + 1) * C, l * C : (l + 1) * C] = pw_ref[...]
-    step = 384
     copies = []
-    for i in range(HALF // step):
-        cols = slice(i * step, (i + 1) * step)
+    for lo, hi in zip(EDGES[:-1], EDGES[1:]):
+        cols = slice(lo, hi)
         even = dot(lhs_ref[:, :256], t_ref[:256, cols], NN)
         odd = dot(lhs_ref[:, 256:], t_ref[256:, cols], NN)
         for h, spec in enumerate((even + odd, even - odd)):
-            cols = slice(h * HALF + i * step, h * HALF + (i + 1) * step)
+            cols = slice(h * HALF + lo, h * HALF + hi)
             out_ref[:, cols] = (spec + dot(pd_ref[...], dz_ref[:, cols], NN)).astype(bf16)
-            copies.append(pltpu.make_async_copy(out_ref.at[:, cols], out_hbm.at[:, cols], sems.at[2 * i + h]))
+            copies.append(pltpu.make_async_copy(out_ref.at[:, cols], out_hbm.at[:, cols], sems.at[len(copies)]))
             copies[-1].start()
     for copy in copies:
         copy.wait()
@@ -311,6 +334,7 @@
         ),
         [
             pltpu.VMEM((HALF, SLOTS), bf16),
+            pltpu.VMEM((512, SLOTS), bf16),
             pltpu.VMEM((ROWS_DEV, 512, 128), f32),
             pltpu.VMEM((LC, NX), bf16),
             pltpu.VMEM((2 * LC, HALF), bf16),
@@ -338,6 +362,26 @@
     )
 
 
+def grad_call(msg, table, dz, point_weight):
+    return call(
+        grad_kernel,
+        jax.ShapeDtypeStruct((LC, NX), bf16),
+        [
+            pltpu.VMEM((ROWS_DEV, 256, 128), f32),
+            pltpu.VMEM((LC, 512), bf16),
+            pltpu.VMEM((LC, LC), bf16),
+            pltpu.VMEM((LC, NX), bf16),
+            pltpu.SemaphoreType.DMA((2 * len(EDGES),)),
+        ],
+        2 * LC * NX * 448,
+        msg,
+        table,
+        dz,
+        point_weight,
+        out_specs=FAR,
+    )
+
+
 def local(inputs, preact, spectral_weight, point_weight, readout, observed, cell_index, drift_steps, counts):
     table = jnp.asarray(lon_table())
     lat = jnp.asarray(lat_table())
@@ -390,23 +434,7 @@
         lat,
     )
     msg = lax.all_to_all(msg, "domain", 0, 0, tiled=True)
-    input_grad = call(
-        grad_kernel,
-        jax.ShapeDtypeStruct((LC, NX), bf16),
-        [
-            pltpu.VMEM((ROWS_DEV, 256, 128), f32),
-            pltpu.VMEM((LC, 512), bf16),
-            pltpu.VMEM((LC, LC), bf16),
-            pltpu.VMEM((LC, NX), bf16),
-            pltpu.SemaphoreType.DMA((6,)),
-        ],
-        2 * LC * NX * 448,
-        msg,
-        table,
-        dz,
-        point_weight,
-        out_specs=FAR,
-    )
+    input_grad = grad_call(msg, table, dz, point_weight)
     return (input_grad.reshape(1, ROWS_DEV, C, NX), weight_grad)
 
 

time: 86.8 us -> 86.3 us (level)
  no operation moved by 1% of the time
where the time goes in v5:
time: 86.3 us; the launch traced here: 86 us
  blocking collectives  60.8 us (70%)
  Pallas kernels  10.3 us (12%)
  waiting for transfers between devices  8.39 us (10%)
  starting transfers between devices  5.13 us (6%)
  between operations  1.36 us (2%)
    all_to_all x1, blocking collectives, local(): msg = lax.all_to_all(msg, 'domain', 0, 0, tiled=True)  30.5 us
    all_to_all x1, blocking collectives, local(): modes = lax.all_to_all(modes, 'dp', 0, 0, tiled=True)  17.2 us
    all_to_all x1, blocking collectives, local(): dmodes = lax.all_to_all(dmodes, 'dp', 0, 0, tiled=True)  13.1 us
    pallas_call x7, Pallas kernels, call(): pl.pallas_call(kernel, out_shape=outs, in_specs=specs or [WHOLE] * len(ar...  10.3 us
    all_to_all x1, waiting for transfers between devices, local(): msg = lax.all_to_all(msg, 'domain', 0, 0, tiled=True)  8.39 us
    all_to_all x1, starting transfers between devices, local(): msg = lax.all_to_all(msg, 'domain', 0, 0, tiled=True)  5.13 us
  transfers between devices with their start and end apart: 1, of which 1 were waited for; matrix products, arithmetic and copies ran while one was open for 0% of the time, Pallas kernels for 3%

profile of v5, /device:TPU:8, one launch (start us, length us, event | category | flops | bytes accessed | tf_op | source)
XLA Modules:
  0.0 86.0 jit_solution(17726573543655327922)
XLA Ops:
  1.3 0.0 copy-start
  1.3 0.0 copy-start.2
  1.3 3.6 %shard_map.122 = (bf16[64,8,384]{2,1,0:T(8,128)(2,1)S(1)}, f32[64,512]{1,0:T(8,128)S(1)}) custom-call(bf16[192,2304]{1,0:T(8,128)(2,1)} %bitcast.5, bf16[192,2304]{1,0:T(8,128)(2,1)} %bitcast.6, bf16[512,1152]{1,0:T(8,128)(2,1)} %constant.4.clone.t_hbm.t_ref, f32[48,2,64]{2,1,0:T(2,128)} %ro_hbm.1, f32[2,512]{1,0:T(2,128)} %bitcast.7, s32[1,512]{1,0:T(1,128)} %cell_ref.1, ...), custom_call_target="tpu_custom_call" | custom-call | flops 1811939328 | bytes 2981892 | tf_op jit(solution)/shard_map/pallas_call | solution.py:316
  4.9 30.5 %all_to_all.20.msg_ref = bf16[64,8,384]{2,1,0:T(8,128)(2,1)S(1)} all-to-all(bf16[64,8,384]{2,1,0:T(8,128)(2,1)S(1)} %get-tuple-element.6), channel_id=1, replica_groups=mesh['dp'=8,'domain'=64] {'domain'}, dimensions={0} | all-to-all | bytes 786432 | tf_op jit(solution)/shard_map/all_to_all | solution.py:389
  35.4 0.0 copy-done
  35.4 0.0 copy-done.2
  35.4 0.5 shard_map.123
  35.8 17.2 %all_to_all.21.modes_ref = bf16[8,128,128]{2,1,0:T(8,128)(2,1)S(1)} all-to-all(bf16[8,128,128]{2,1,0:T(8,128)(2,1)S(1)} %shard_map.123), channel_id=1, replica_groups=mesh['dp'=8,'domain'=64] {'dp'}, dimensions={0} | all-to-all | bytes 524288 | tf_op jit(solution)/shard_map/all_to_all | solution.py:399
  53.1 0.0 copy-start.4
  53.1 0.8 shard_map.124
  53.8 13.1 %all_to_all.22.modes_ref = bf16[8,64,128]{2,1,0:T(8,128)(2,1)S(1)} all-to-all(bf16[8,64,128]{2,1,0:T(8,128)(2,1)S(1)} %get-tuple-element.7), channel_id=1, replica_groups=mesh['dp'=8,'domain'=64] {'dp'}, dimensions={0} | all-to-all | bytes 262144 | tf_op jit(solution)/shard_map/all_to_all | solution.py:409
  66.9 1.0 %shard_map.125 = bf16[64,4,384]{2,1,0:T(4,128)(2,1)} custom-call(bf16[8,64,128]{2,1,0:T(8,128)(2,1)S(1)} %all_to_all.22.modes_ref, bf16[256,384]{1,0:T(8,128)(2,1)S(1)} %get-tuple-element.8.m_ref), custom_call_target="tpu_custom_call" | custom-call | flops 50331648 | bytes 327680 | tf_op jit(solution)/shard_map/pallas_call | solution.py:316
  67.9 5.1 %all-to-all-start.3 = ((bf16[64,4,384]{2,1,0:T(4,128)(2,1)}), bf16[64,4,384]{2,1,0:T(4,128)(2,1)S(1)}, u32[]{:S(2)}, u32[]{:S(2)}) async-start(bf16[64,4,384]{2,1,0:T(4,128)(2,1)} %shard_map.125), calls=%async_computation.3 | async-start | bytes 393216 | tf_op jit(solution)/shard_map/all_to_all | solution.py:436
  73.0 0.0 copy-done.4
  73.0 1.1 %shard_map.126.dz_ref = bf16[192,2304]{1,0:T(8,128)(2,1)S(1)} custom-call(f32[64,512]{1,0:T(8,128)S(1)} %get-tuple-element.9.dslot_ref, s32[1,512]{1,0:T(1,128)S(1)} %copy-done.4), custom_call_target="tpu_custom_call" | custom-call | flops 905969664 | bytes 133120 | tf_op jit(solution)/shard_map/pallas_call | solution.py:316
  74.2 0.0 copy-start.1
  74.2 0.0 copy-start.3
  74.2 1.8 %shard_map.128 = bf16[16,4,64,128]{3,2,1,0:T(8,128)(2,1)} custom-call(bf16[8,128,128]{2,1,0:T(8,128)(2,1)S(1)} %all_to_all.21.modes_ref), custom_call_target="tpu_custom_call" | custom-call | flops 268435456 | bytes 262144 | tf_op jit(solution)/shard_map/pallas_call | solution.py:316
  76.1 8.4 %all-to-all-done.3.msg_ref = bf16[64,4,384]{2,1,0:T(4,128)(2,1)S(1)} async-done(((bf16[64,4,384]{2,1,0:T(4,128)(2,1)}), bf16[64,4,384]{2,1,0:T(4,128)(2,1)S(1)}, u32[]{:S(2)}, u32[]{:S(2)}) %all-to-all-start.3) | async-done | bytes 196640 | tf_op jit(solution)/shard_map/all_to_all | solution.py:436
  84.4 0.0 copy-done.1
  84.4 0.0 copy-done.3
  84.5 1.5 %shard_map.127 = bf16[192,2304]{1,0:T(8,128)(2,1)} custom-call(bf16[64,4,384]{2,1,0:T(4,128)(2,1)S(1)} %all-to-all-done.3.msg_ref, bf16[512,1152]{1,0:T(8,128)(2,1)S(1)} %copy-done.1, bf16[192,2304]{1,0:T(8,128)(2,1)S(1)} %shard_map.126.dz_ref, bf16[64,64]{1,0:T(8,128)(2,1)S(1)} %copy-done.3), custom_call_target="tpu_custom_call" | custom-call | flops 396361728 | bytes 2269184 | tf_op jit(solution)/shard_map/pallas_call | solution.py:316
Async XLA Ops:
  1.3 34.1 %copy-start = (bf16[16,4,64,128]{3,2,1,0:T(8,128)(2,1)S(1)}, bf16[16,4,64,128]{3,2,1,0:T(8,128)(2,1)}, u32[]{:S(2)}) copy-start(bf16[16,4,64,128]{3,2,1,0:T(8,128)(2,1)} %w_ref.3) | copy-start | bytes 3145732
  1.3 34.1 %copy-start.2 = (bf16[256,384]{1,0:T(8,128)(2,1)S(1)}, bf16[256,384]{1,0:T(8,128)(2,1)}, u32[]{:S(2)}) copy-start(bf16[256,384]{1,0:T(8,128)(2,1)} %constant.5.clone.m_ref) | copy-start | bytes 589828
  53.1 20.0 %copy-start.4 = (s32[1,512]{1,0:T(1,128)S(1)}, s32[1,512]{1,0:T(1,128)}, u32[]{:S(2)}) copy-start(s32[1,512]{1,0:T(1,128)} %cell_ref.1) | copy-start | bytes 6148
  67.9 16.5 %all-to-all-start.3 = ((bf16[64,4,384]{2,1,0:T(4,128)(2,1)}), bf16[64,4,384]{2,1,0:T(4,128)(2,1)S(1)}, u32[]{:S(2)}, u32[]{:S(2)}) async-start(bf16[64,4,384]{2,1,0:T(4,128)(2,1)} %shard_map.125), calls=%async_computation.3 | async-start | bytes 393216 | tf_op jit(solution)/shard_map/all_to_all | solution.py:436
  74.2 10.3 %copy-start.1 = (bf16[512,1152]{1,0:T(8,128)(2,1)S(1)}, bf16[512,1152]{1,0:T(8,128)(2,1)}, u32[]{:S(2)}) copy-start(bf16[512,1152]{1,0:T(8,128)(2,1)} %constant.4.clone.t_hbm.t_ref) | copy-start | bytes 3538948
  74.2 10.3 %copy-start.3 = (bf16[64,64]{1,0:T(8,128)(2,1)S(1)}, bf16[64,64]{1,0:T(8,128)(2,1)}, u32[]{:S(2)}) copy-start(bf16[64,64]{1,0:T(8,128)(2,1)} %pw_ref.1) | copy-start | bytes 24580

commit v6 on v5

--- a/solution.py
+++ b/solution.py
@@ -110,7 +110,7 @@
 
 
 def slots_kernel(
-    x_hbm, p_hbm, t_hbm, ro_hbm, obs_hbm, cell_hbm, step_hbm, cnt_ref, msg_ref, dslot_ref, oh_ref, wave_ref, sc_ref, x_ref, p_ref, t_ref, ro_ref, obs_ref, cell_ref, step_ref, sems,
+    x_hbm, p_hbm, t_hbm, ro_hbm, obs_hbm, cell_hbm, step_hbm, w_hbm, m_hbm, cnt_ref, msg_ref, dslot_ref, w_ref, m_ref, oh_ref, wave_ref, sc_ref, x_ref, p_ref, t_ref, ro_ref, obs_ref, cell_ref, step_ref, sems,
 ):
     moves = (
         (cell_hbm, cell_ref),
@@ -121,6 +121,8 @@
         (p_hbm.at[:, HALF:], p_ref.at[LC:]),
         (t_hbm, t_ref),
         (x_hbm, x_ref),
+        (m_hbm, m_ref),
+        (w_hbm, w_ref),
     )
     copies = [pltpu.make_async_copy(src, dst, sems.at[i]) for i, (src, dst) in enumerate(moves)]
     for copy in copies:
@@ -180,6 +182,8 @@
     place_spectra(1, *[spec[:, :LC] + spec[:, LC:] for spec in parts])
     for l in range(ROWS_DEV):
         msg_ref[:, :, l * 128 : (l + 1) * 128] = sc_ref[l].reshape(N_DOMAIN, 8, 128).astype(bf16)
+    copies[8].wait()
+    copies[9].wait()
 
 
 def scatter_kernel(dslot_ref, cell_ref, dz_ref, oh_ref):
@@ -192,8 +196,7 @@
         dz_ref[:, i * step : (i + 1) * step] = (grid[:LC] + grid[LC:]).astype(bf16)
 
 
-def lat_kernel(msg_ref, m_ref, w_ref, out_ref, sc_ref, rhs_ref):
-    del w_ref
+def lat_kernel(msg_ref, m_ref, out_ref, sc_ref, rhs_ref):
     for l in range(ROWS_DEV):
         sc_ref[l] = msg_ref[:, :, l * 128 : (l + 1) * 128].astype(f32).reshape(N_DOMAIN * 8, 128)
     for xz in range(2):
@@ -324,13 +327,15 @@
     )(*args)
 
 
-def slots_call(inputs, preact, table, readout, observed, cell_index, drift_steps, counts):
+def slots_call(inputs, preact, table, readout, observed, cell_index, drift_steps, counts, weight, lat):
     small = [pltpu.VMEM((1, SLOTS), jnp.int32), pltpu.VMEM((1, SLOTS), jnp.int32)]
     return call(
         slots_kernel,
         (
             jax.ShapeDtypeStruct((N_DOMAIN, 8, 384), bf16),
             jax.ShapeDtypeStruct((C, SLOTS), f32),
+            jax.ShapeDtypeStruct(weight.shape, bf16),
+            jax.ShapeDtypeStruct(lat.shape, bf16),
         ),
         [
             pltpu.VMEM((HALF, SLOTS), bf16),
@@ -342,7 +347,7 @@
             pltpu.VMEM((STEPS, 2, C), f32),
             pltpu.VMEM((2, SLOTS), f32),
             *small,
-            pltpu.SemaphoreType.DMA((8,)),
+            pltpu.SemaphoreType.DMA((10,)),
         ],
         2 * LC * NX * 512 * 4,
         *[
@@ -355,10 +360,12 @@
                 observed.reshape(2, SLOTS),
                 cell_index,
                 drift_steps,
+                weight,
+                lat,
             )
         ],
         counts,
-        specs=[FAR] * 7 + [pl.BlockSpec(memory_space=pltpu.SMEM)],
+        specs=[FAR] * 9 + [pl.BlockSpec(memory_space=pltpu.SMEM)],
     )
 
 
@@ -385,7 +392,9 @@
 def local(inputs, preact, spectral_weight, point_weight, readout, observed, cell_index, drift_steps, counts):
     table = jnp.asarray(lon_table())
     lat = jnp.asarray(lat_table())
-    msg, dslot = slots_call(inputs, preact, table, readout, observed, cell_index, drift_steps, counts)
+    msg, dslot, weight, lat = slots_call(
+        inputs, preact, table, readout, observed, cell_index, drift_steps, counts, spectral_weight, lat
+    )
     msg = lax.all_to_all(msg, "domain", 0, 0, tiled=True)
     modes = call(
         lat_kernel,
@@ -394,7 +403,6 @@
         2 * 256 * 384 * 512,
         msg,
         lat,
-        spectral_weight,
     )
     modes = lax.all_to_all(modes, "dp", 0, 0, tiled=True)
     dmodes, lat = call(
@@ -403,7 +411,7 @@
         [pltpu.VMEM((512, 128), f32), pltpu.VMEM((512, 128), f32)],
         2 * 32 * 128 * 128 * 256,
         modes,
-        spectral_weight,
+        weight,
         lat,
     )
     dmodes = lax.all_to_all(dmodes, "dp", 0, 0, tiled=True)

time: 86.3 us -> 86.2 us (level)
  no operation moved by 1% of the time
where the time goes in v6:
time: 86.2 us; the launch traced here: 85.9 us
  blocking collectives  60.8 us (71%)
  Pallas kernels  10.2 us (12%)
  waiting for transfers between devices  8.39 us (10%)
  starting transfers between devices  5.13 us (6%)
  between operations  1.35 us (2%)
    all_to_all x1, blocking collectives, local(): msg = lax.all_to_all(msg, 'domain', 0, 0, tiled=True)  30.5 us
    all_to_all x1, blocking collectives, local(): modes = lax.all_to_all(modes, 'dp', 0, 0, tiled=True)  17.2 us
    all_to_all x1, blocking collectives, local(): dmodes = lax.all_to_all(dmodes, 'dp', 0, 0, tiled=True)  13.1 us
    pallas_call x7, Pallas kernels, call(): pl.pallas_call(kernel, out_shape=outs, in_specs=specs or [WHOLE] * len(ar...  10.2 us
    all_to_all x1, waiting for transfers between devices, local(): msg = lax.all_to_all(msg, 'domain', 0, 0, tiled=True)  8.39 us
    all_to_all x1, starting transfers between devices, local(): msg = lax.all_to_all(msg, 'domain', 0, 0, tiled=True)  5.13 us
  transfers between devices with their start and end apart: 1, of which 1 were waited for; matrix products, arithmetic and copies ran while one was open for 0% of the time, Pallas kernels for 3%

profile of v6, /device:TPU:8, one launch (start us, length us, event | category | flops | bytes accessed | tf_op | source)
XLA Modules:
  0.0 85.9 jit_solution(13741495092605799402)
XLA Ops:
  1.3 3.5 %shard_map.122 = (bf16[64,8,384]{2,1,0:T(8,128)(2,1)S(1)}, f32[64,512]{1,0:T(8,128)S(1)}, bf16[16,4,64,128]{3,2,1,0:T(8,128)(2,1)S(1)}, bf16[256,384]{1,0:T(8,128)(2,1)S(1)}) custom-call(bf16[192,2304]{1,0:T(8,128)(2,1)} %bitcast.5, bf16[192,2304]{1,0:T(8,128)(2,1)} %bitcast.6, bf16[512,1152]{1,0:T(8,128)(2,1)} %constant.4.clone.t_hbm.t_ref, ...), custom_call_target="tpu_custom_call" | custom-call | flops 1811939328 | bytes 4227076 | tf_op jit(solution)/shard_map/pallas_call | solution.py:319
  4.8 30.5 %all_to_all.20.msg_ref = bf16[64,8,384]{2,1,0:T(8,128)(2,1)S(1)} all-to-all(bf16[64,8,384]{2,1,0:T(8,128)(2,1)S(1)} %get-tuple-element.8), channel_id=1, replica_groups=mesh['dp'=8,'domain'=64] {'domain'}, dimensions={0} | all-to-all | bytes 786432 | tf_op jit(solution)/shard_map/all_to_all | solution.py:398
  35.3 0.5 shard_map.123
  35.7 17.2 %all_to_all.21.modes_ref = bf16[8,128,128]{2,1,0:T(8,128)(2,1)S(1)} all-to-all(bf16[8,128,128]{2,1,0:T(8,128)(2,1)S(1)} %shard_map.123), channel_id=1, replica_groups=mesh['dp'=8,'domain'=64] {'dp'}, dimensions={0} | all-to-all | bytes 524288 | tf_op jit(solution)/shard_map/all_to_all | solution.py:407
  53.0 0.0 copy-start.2
  53.0 0.8 shard_map.124
  53.7 13.1 %all_to_all.22.modes_ref = bf16[8,64,128]{2,1,0:T(8,128)(2,1)S(1)} all-to-all(bf16[8,64,128]{2,1,0:T(8,128)(2,1)S(1)} %get-tuple-element.11), channel_id=1, replica_groups=mesh['dp'=8,'domain'=64] {'dp'}, dimensions={0} | all-to-all | bytes 262144 | tf_op jit(solution)/shard_map/all_to_all | solution.py:417
  66.8 1.0 %shard_map.125 = bf16[64,4,384]{2,1,0:T(4,128)(2,1)} custom-call(bf16[8,64,128]{2,1,0:T(8,128)(2,1)S(1)} %all_to_all.22.modes_ref, bf16[256,384]{1,0:T(8,128)(2,1)S(1)} %get-tuple-element.12.m_ref), custom_call_target="tpu_custom_call" | custom-call | flops 50331648 | bytes 327680 | tf_op jit(solution)/shard_map/pallas_call | solution.py:319
  67.8 5.1 %all-to-all-start.3 = ((bf16[64,4,384]{2,1,0:T(4,128)(2,1)}), bf16[64,4,384]{2,1,0:T(4,128)(2,1)S(1)}, u32[]{:S(2)}, u32[]{:S(2)}) async-start(bf16[64,4,384]{2,1,0:T(4,128)(2,1)} %shard_map.125), calls=%async_computation.3 | async-start | bytes 393216 | tf_op jit(solution)/shard_map/all_to_all | solution.py:444
  72.9 0.0 copy-done.2
  72.9 1.1 %shard_map.126.dz_ref = bf16[192,2304]{1,0:T(8,128)(2,1)S(1)} custom-call(f32[64,512]{1,0:T(8,128)S(1)} %get-tuple-element.13.dslot_ref, s32[1,512]{1,0:T(1,128)S(1)} %copy-done.2), custom_call_target="tpu_custom_call" | custom-call | flops 905969664 | bytes 133120 | tf_op jit(solution)/shard_map/pallas_call | solution.py:319
  74.1 0.0 copy-start
  74.1 0.0 copy-start.1
  74.1 1.8 %shard_map.128 = bf16[16,4,64,128]{3,2,1,0:T(8,128)(2,1)} custom-call(bf16[8,128,128]{2,1,0:T(8,128)(2,1)S(1)} %all_to_all.21.modes_ref), custom_call_target="tpu_custom_call" | custom-call | flops 268435456 | bytes 262144 | tf_op jit(solution)/shard_map/pallas_call | solution.py:319
  75.9 8.4 %all-to-all-done.3.msg_ref = bf16[64,4,384]{2,1,0:T(4,128)(2,1)S(1)} async-done(((bf16[64,4,384]{2,1,0:T(4,128)(2,1)}), bf16[64,4,384]{2,1,0:T(4,128)(2,1)S(1)}, u32[]{:S(2)}, u32[]{:S(2)}) %all-to-all-start.3) | async-done | bytes 196640 | tf_op jit(solution)/shard_map/all_to_all | solution.py:444
  84.3 0.0 copy-done
  84.3 0.0 copy-done.1
  84.3 1.5 %shard_map.127 = bf16[192,2304]{1,0:T(8,128)(2,1)} custom-call(bf16[64,4,384]{2,1,0:T(4,128)(2,1)S(1)} %all-to-all-done.3.msg_ref, bf16[512,1152]{1,0:T(8,128)(2,1)S(1)} %copy-done, bf16[192,2304]{1,0:T(8,128)(2,1)S(1)} %shard_map.126.dz_ref, bf16[64,64]{1,0:T(8,128)(2,1)S(1)} %copy-done.1), custom_call_target="tpu_custom_call" | custom-call | flops 396361728 | bytes 2269184 | tf_op jit(solution)/shard_map/pallas_call | solution.py:319
Async XLA Ops:
  53.0 20.0 %copy-start.2 = (s32[1,512]{1,0:T(1,128)S(1)}, s32[1,512]{1,0:T(1,128)}, u32[]{:S(2)}) copy-start(s32[1,512]{1,0:T(1,128)} %cell_ref.1) | copy-start | bytes 6148
  67.8 16.5 %all-to-all-start.3 = ((bf16[64,4,384]{2,1,0:T(4,128)(2,1)}), bf16[64,4,384]{2,1,0:T(4,128)(2,1)S(1)}, u32[]{:S(2)}, u32[]{:S(2)}) async-start(bf16[64,4,384]{2,1,0:T(4,128)(2,1)} %shard_map.125), calls=%async_computation.3 | async-start | bytes 393216 | tf_op jit(solution)/shard_map/all_to_all | solution.py:444
  74.1 10.3 %copy-start = (bf16[512,1152]{1,0:T(8,128)(2,1)S(1)}, bf16[512,1152]{1,0:T(8,128)(2,1)}, u32[]{:S(2)}) copy-start(bf16[512,1152]{1,0:T(8,128)(2,1)} %constant.4.clone.t_hbm.t_ref) | copy-start | bytes 3538948
  74.1 10.3 %copy-start.1 = (bf16[64,64]{1,0:T(8,128)(2,1)S(1)}, bf16[64,64]{1,0:T(8,128)(2,1)}, u32[]{:S(2)}) copy-start(bf16[64,64]{1,0:T(8,128)(2,1)} %pw_ref.1) | copy-start | bytes 24580

commit v7 on v6

--- a/solution.py
+++ b/solution.py
@@ -271,7 +271,7 @@
                 out_ref[ql, kh * 2 + kl] = jnp.concatenate([re, im], axis=1).astype(bf16)
 
 
-def synth_kernel(modes_ref, m_ref, out_ref, d_ref, sc_ref):
+def synth_kernel(modes_ref, m_ref, out_hbm, d_ref, sc_ref, out_ref, sems):
     for q in range(N_DP):
         for kh in range(2):
             d_ref[q * 32 : (q + 1) * 32, kh * 128 : (kh + 1) * 128] = modes_ref[q, kh * 32 : (kh + 1) * 32, :]
@@ -282,8 +282,14 @@
             for kh in range(2):
                 block = lat[at : at + N_DOMAIN, kh * 128 : (kh + 1) * 128]
                 sc_ref[l, pl.ds(part * 2 + kh, N_DOMAIN, stride=4), :] = block
+    copies = []
     for l in range(ROWS_DEV):
-        out_ref[:, :, l * 128 : (l + 1) * 128] = sc_ref[l].reshape(N_DOMAIN, 4, 128).astype(bf16)
+        lanes = slice(l * 128, (l + 1) * 128)
+        out_ref[:, :, lanes] = sc_ref[l].reshape(N_DOMAIN, 4, 128).astype(bf16)
+        copies.append(pltpu.make_async_copy(out_ref.at[:, :, lanes], out_hbm.at[:, :, lanes], sems.at[l]))
+        copies[-1].start()
+    for copy in copies:
+        copy.wait()
 
 
 def grad_kernel(msg_ref, t_ref, dz_ref, pw_ref, out_hbm, sc_ref, lhs_ref, pd_ref, out_ref, sems):
@@ -432,14 +438,17 @@
     )
     msg = call(
         synth_kernel,
-        jax.ShapeDtypeStruct((N_DOMAIN, 4, 384), bf16),
+        pltpu.HBM((N_DOMAIN, 4, 384), bf16),
         [
             pltpu.VMEM((256, 256), bf16),
             pltpu.VMEM((ROWS_DEV, 256, 128), f32),
+            pltpu.VMEM((N_DOMAIN, 4, 384), bf16),
+            pltpu.SemaphoreType.DMA((ROWS_DEV,)),
         ],
         2 * 256 * 384 * 256,
         dmodes,
         lat,
+        out_specs=FAR,
     )
     msg = lax.all_to_all(msg, "domain", 0, 0, tiled=True)
     input_grad = grad_call(msg, table, dz, point_weight)

time: 86.2 us -> 86.2 us (level)
  no operation moved by 1% of the time
where the time goes in v7:
time: 86.2 us; the launch traced here: 86 us
  blocking collectives  60.8 us (71%)
  Pallas kernels  10.2 us (12%)
  waiting for transfers between devices  8.39 us (10%)
  starting transfers between devices  5.14 us (6%)
  between operations  1.35 us (2%)
    all_to_all x1, blocking collectives, local(): msg = lax.all_to_all(msg, 'domain', 0, 0, tiled=True)  30.5 us
    all_to_all x1, blocking collectives, local(): modes = lax.all_to_all(modes, 'dp', 0, 0, tiled=True)  17.2 us
    all_to_all x1, blocking collectives, local(): dmodes = lax.all_to_all(dmodes, 'dp', 0, 0, tiled=True)  13.1 us
    pallas_call x7, Pallas kernels, call(): pl.pallas_call(kernel, out_shape=outs, in_specs=specs or [WHOLE] * len(ar...  10.2 us
    all_to_all x1, waiting for transfers between devices, local(): msg = lax.all_to_all(msg, 'domain', 0, 0, tiled=True)  8.39 us
    all_to_all x1, starting transfers between devices, local(): msg = lax.all_to_all(msg, 'domain', 0, 0, tiled=True)  5.14 us
  transfers between devices with their start and end apart: 1, of which 1 were waited for; matrix products, arithmetic and copies ran while one was open for 0% of the time, Pallas kernels for 3%

profile of v7, /device:TPU:8, one launch (start us, length us, event | category | flops | bytes accessed | tf_op | source)
XLA Modules:
  0.0 86.0 jit_solution(2216697122005887238)
XLA Ops:
  1.3 3.5 %shard_map.122 = (bf16[64,8,384]{2,1,0:T(8,128)(2,1)S(1)}, f32[64,512]{1,0:T(8,128)S(1)}, bf16[16,4,64,128]{3,2,1,0:T(8,128)(2,1)S(1)}, bf16[256,384]{1,0:T(8,128)(2,1)S(1)}) custom-call(bf16[192,2304]{1,0:T(8,128)(2,1)} %bitcast.5, bf16[192,2304]{1,0:T(8,128)(2,1)} %bitcast.6, bf16[512,1152]{1,0:T(8,128)(2,1)} %constant.4.clone.t_hbm.t_ref, ...), custom_call_target="tpu_custom_call" | custom-call | flops 1811939328 | bytes 4227076 | tf_op jit(solution)/shard_map/pallas_call | solution.py:325
  4.8 30.5 %all_to_all.20.msg_ref = bf16[64,8,384]{2,1,0:T(8,128)(2,1)S(1)} all-to-all(bf16[64,8,384]{2,1,0:T(8,128)(2,1)S(1)} %get-tuple-element.8), channel_id=1, replica_groups=mesh['dp'=8,'domain'=64] {'domain'}, dimensions={0} | all-to-all | bytes 786432 | tf_op jit(solution)/shard_map/all_to_all | solution.py:404
  35.3 0.5 shard_map.123
  35.7 17.2 %all_to_all.21.modes_ref = bf16[8,128,128]{2,1,0:T(8,128)(2,1)S(1)} all-to-all(bf16[8,128,128]{2,1,0:T(8,128)(2,1)S(1)} %shard_map.123), channel_id=1, replica_groups=mesh['dp'=8,'domain'=64] {'dp'}, dimensions={0} | all-to-all | bytes 524288 | tf_op jit(solution)/shard_map/all_to_all | solution.py:413
  53.0 0.0 copy-start.2
  53.0 0.8 shard_map.124
  53.8 13.1 %all_to_all.22.modes_ref = bf16[8,64,128]{2,1,0:T(8,128)(2,1)S(1)} all-to-all(bf16[8,64,128]{2,1,0:T(8,128)(2,1)S(1)} %get-tuple-element.11), channel_id=1, replica_groups=mesh['dp'=8,'domain'=64] {'dp'}, dimensions={0} | all-to-all | bytes 262144 | tf_op jit(solution)/shard_map/all_to_all | solution.py:423
  66.9 1.0 %shard_map.125 = bf16[64,4,384]{2,1,0:T(4,128)(2,1)} custom-call(bf16[8,64,128]{2,1,0:T(8,128)(2,1)S(1)} %all_to_all.22.modes_ref, bf16[256,384]{1,0:T(8,128)(2,1)S(1)} %get-tuple-element.12.m_ref), custom_call_target="tpu_custom_call" | custom-call | flops 50331648 | bytes 327680 | tf_op jit(solution)/shard_map/pallas_call | solution.py:325
  67.8 5.1 %all-to-all-start.3 = ((bf16[64,4,384]{2,1,0:T(4,128)(2,1)}), bf16[64,4,384]{2,1,0:T(4,128)(2,1)S(1)}, u32[]{:S(2)}, u32[]{:S(2)}) async-start(bf16[64,4,384]{2,1,0:T(4,128)(2,1)} %shard_map.125), calls=%async_computation.3 | async-start | bytes 393216 | tf_op jit(solution)/shard_map/all_to_all | solution.py:453
  73.0 0.0 copy-done.2
  73.0 1.1 %shard_map.126.dz_ref = bf16[192,2304]{1,0:T(8,128)(2,1)S(1)} custom-call(f32[64,512]{1,0:T(8,128)S(1)} %get-tuple-element.13.dslot_ref, s32[1,512]{1,0:T(1,128)S(1)} %copy-done.2), custom_call_target="tpu_custom_call" | custom-call | flops 905969664 | bytes 133120 | tf_op jit(solution)/shard_map/pallas_call | solution.py:325
  74.1 0.0 copy-start
  74.1 0.0 copy-start.1
  74.1 1.8 %shard_map.128 = bf16[16,4,64,128]{3,2,1,0:T(8,128)(2,1)} custom-call(bf16[8,128,128]{2,1,0:T(8,128)(2,1)S(1)} %all_to_all.21.modes_ref), custom_call_target="tpu_custom_call" | custom-call | flops 268435456 | bytes 262144 | tf_op jit(solution)/shard_map/pallas_call | solution.py:325
  76.0 8.4 %all-to-all-done.3.msg_ref = bf16[64,4,384]{2,1,0:T(4,128)(2,1)S(1)} async-done(((bf16[64,4,384]{2,1,0:T(4,128)(2,1)}), bf16[64,4,384]{2,1,0:T(4,128)(2,1)S(1)}, u32[]{:S(2)}, u32[]{:S(2)}) %all-to-all-start.3) | async-done | bytes 196640 | tf_op jit(solution)/shard_map/all_to_all | solution.py:453
  84.4 0.0 copy-done
  84.4 0.0 copy-done.1
  84.4 1.6 %shard_map.127 = bf16[192,2304]{1,0:T(8,128)(2,1)} custom-call(bf16[64,4,384]{2,1,0:T(4,128)(2,1)S(1)} %all-to-all-done.3.msg_ref, bf16[512,1152]{1,0:T(8,128)(2,1)S(1)} %copy-done, bf16[192,2304]{1,0:T(8,128)(2,1)S(1)} %shard_map.126.dz_ref, bf16[64,64]{1,0:T(8,128)(2,1)S(1)} %copy-done.1), custom_call_target="tpu_custom_call" | custom-call | flops 396361728 | bytes 2269184 | tf_op jit(solution)/shard_map/pallas_call | solution.py:325
Async XLA Ops:
  53.0 20.0 %copy-start.2 = (s32[1,512]{1,0:T(1,128)S(1)}, s32[1,512]{1,0:T(1,128)}, u32[]{:S(2)}) copy-start(s32[1,512]{1,0:T(1,128)} %cell_ref.1) | copy-start | bytes 6148
  67.8 16.6 %all-to-all-start.3 = ((bf16[64,4,384]{2,1,0:T(4,128)(2,1)}), bf16[64,4,384]{2,1,0:T(4,128)(2,1)S(1)}, u32[]{:S(2)}, u32[]{:S(2)}) async-start(bf16[64,4,384]{2,1,0:T(4,128)(2,1)} %shard_map.125), calls=%async_computation.3 | async-start | bytes 393216 | tf_op jit(solution)/shard_map/all_to_all | solution.py:453
  74.1 10.3 %copy-start = (bf16[512,1152]{1,0:T(8,128)(2,1)S(1)}, bf16[512,1152]{1,0:T(8,128)(2,1)}, u32[]{:S(2)}) copy-start(bf16[512,1152]{1,0:T(8,128)(2,1)} %constant.4.clone.t_hbm.t_ref) | copy-start | bytes 3538948
  74.1 10.3 %copy-start.1 = (bf16[64,64]{1,0:T(8,128)(2,1)S(1)}, bf16[64,64]{1,0:T(8,128)(2,1)}, u32[]{:S(2)}) copy-start(bf16[64,64]{1,0:T(8,128)(2,1)} %pw_ref.1) | copy-start | bytes 24580
